TPU v7x, 256 devices: a whole 4x4x8 slice. The times are simulated.
256 devices in a mesh: cp: 32 (over x_hi, z, core), tp: 4 (over y), dp: 2 (over x_lo).
Axes of the slice: x: 4 (x_hi: 2, x_lo: 2; x = x_hi * 2 + x_lo), y: 4, z: 8, core: 2. Of those that a mesh axis runs over, the one named last changes fastest.
Arguments:
- query_rows: bfloat16 [2, 4096, 6144], P('dp', 'cp', 'tp'), may hold values from -8 to 8
- key_rows: bfloat16 [2, 4096, 1024], P('dp', 'cp', 'tp'), may hold values from -8 to 8
- value_rows: bfloat16 [2, 4096, 1024], P('dp', 'cp', 'tp'), may hold values from -6 to 6
- attention_out: bfloat16 [2, 4096, 6144], P('dp', 'cp', 'tp'), may hold values from -6 to 6
- output_grad: bfloat16 [2, 4096, 6144], P('dp', 'cp', 'tp'), may hold values from -24 to 24
- log_norms: float32 [2, 4096, 48], P('dp', 'cp', 'tp')
- moe_grad: bfloat16 [2, 4096, 6144], P('dp', 'cp', 'tp'), may hold values from -6 to 6
- expert_ids: int32 [2, 4096, 2], P('dp', 'cp'), may hold values from 0 to 7, all different within a row; in each aligned block of 128 rows (0 to 127, 128 to 255, ..., all dimensions but the last counted through in order) at most 48 rows name the same one
- route_weight: int32 [2, 4096, 2], P('dp', 'cp'), may hold values from 1 to 32767
- hidden_act: bfloat16 [2, 1536, 65536], P('dp', 'tp', 'cp'), may hold values from -0.1875 to 0.1875
Outputs:
- query_grad: bfloat16 [2, 4096, 6144], P('dp', 'cp', 'tp')
- key_grad: bfloat16 [2, 4096, 1024], P('dp', 'cp', 'tp')
- value_grad: bfloat16 [2, 4096, 1024], P('dp', 'cp', 'tp')
- down_grad: bfloat16 [65536, 6144], P(('cp', 'dp'), 'tp')
Inputs may be any that keep to these rules, and one draw needn't show every extreme that they name: `expert_ids`: in each aligned block of 128 tokens of a sequence no expert is named by more than 48 tokens, a bound that some block reaches; a token names 2 different experts.
All inputs are finite; a program needn't handle non-finite values.
Results may differ from a plain program's by a relative error of at most 0.0052.
Values may be sent and summed in bfloat16 or wider, within the bound.
No kernel may reach another device: no remote copies, remote signals or barrier semaphores. Data moves between devices by JAX's collectives and lax.ppermute only.
A program may use at most 128 MiB of HBM per device.

v0:
```python
import jax
import jax.numpy as jnp
from jax import lax
from jax.sharding import PartitionSpec as P

HEADS = 48
KV_HEADS = 8
HEAD_DIM = 128
KEY_BLOCK = 512


ACCURATE = lax.Precision.HIGHEST


def route_slots(chosen_ids, weight_codes, expert_count, capacity, grad_rows):
    expert_axis = jnp.arange(expert_count, dtype=jnp.int32)
    chosen = chosen_ids[:, :, None] == expert_axis[None, None, :]
    route_hits = jnp.sum(chosen.astype(jnp.int32), axis=1)
    slot_rank = jnp.cumsum(route_hits, axis=0) - route_hits
    weights_real = weight_codes.astype(jnp.float32) / 32768.0
    route_scale = jnp.sum(jnp.where(chosen, weights_real[:, :, None], 0.0), axis=1)
    slot_axis = jnp.arange(capacity, dtype=jnp.int32)
    placed = (slot_rank[None, :, :] == slot_axis[:, None, None]) & (route_hits[None, :, :] > 0)
    combine = jnp.where(placed, route_scale[None, :, :], 0.0)
    return jnp.einsum(
        "cte,td->ecd", combine, grad_rows.astype(jnp.float32), precision=ACCURATE
    ).astype(jnp.bfloat16)


def local(
    query_rows,
    key_rows,
    value_rows,
    attention_out,
    output_grad,
    log_norms,
    moe_grad,
    expert_ids,
    route_weight,
    hidden_act,
):
    cp_count = lax.axis_size("cp")
    cp_place = lax.axis_index("cp")
    expert_count = max(4, cp_count // 4)
    spread = cp_count // expert_count
    tokens = query_rows.shape[1]
    capacity = hidden_act.shape[1] * lax.axis_size("tp") // cp_count
    routed = route_slots(expert_ids[0], route_weight[0], expert_count, capacity, moe_grad[0])
    outgoing = jnp.repeat(routed, spread, axis=0)
    arrived = lax.all_to_all(outgoing, "cp", split_axis=0, concat_axis=0, tiled=True)
    arrived = arrived.reshape(cp_count * capacity, arrived.shape[2])
    down_total = lax.dot_general(
        lax.all_gather(hidden_act, "tp", axis=1, tiled=True)[0],
        arrived,
        (((0,), (0,)), ((), ())),
        preferred_element_type=jnp.float32,
    )
    down_grad = lax.psum_scatter(down_total, "dp", scatter_dimension=0, tiled=True).astype(
        jnp.bfloat16
    )
    members = HEADS // KV_HEADS
    kv_width = key_rows.shape[2]
    kv_local = kv_width // HEAD_DIM
    scale_factor = HEAD_DIM ** (-0.5)
    query_four = query_rows[0].reshape(tokens, kv_local, members, HEAD_DIM)
    grad_four = output_grad[0].reshape(tokens, kv_local, members, HEAD_DIM)
    out_four = attention_out[0].reshape(tokens, kv_local, members, HEAD_DIM)
    row_delta = jnp.sum(grad_four.astype(jnp.float32) * out_four.astype(jnp.float32), axis=-1)
    delta_heads = jnp.transpose(row_delta, (1, 2, 0))
    norms_heads = jnp.transpose(log_norms[0].reshape(tokens, kv_local, members), (1, 2, 0))
    gathered = (
        lax.all_gather(key_rows, "cp", axis=1, tiled=True),
        lax.all_gather(value_rows, "cp", axis=1, tiled=True),
    )
    length = gathered[0].shape[1]
    all_keys = gathered[0][0].reshape(length, kv_local, HEAD_DIM)
    all_values = gathered[1][0].reshape(length, kv_local, HEAD_DIM)
    query_pos = cp_place * tokens + jnp.arange(tokens, dtype=jnp.int32)
    blocks_needed = ((cp_place + 1) * tokens + KEY_BLOCK - 1) // KEY_BLOCK

    def block_terms(first_row, row_count):
        key_block = lax.dynamic_slice_in_dim(all_keys, first_row, row_count, 0)
        value_block = lax.dynamic_slice_in_dim(all_values, first_row, row_count, 0)
        scores = (
            jnp.einsum("qkmd,wkd->kmqw", query_four, key_block, preferred_element_type=jnp.float32)
            * scale_factor
        )
        key_pos = first_row + jnp.arange(row_count, dtype=jnp.int32)
        causal = query_pos[:, None] >= key_pos[None, :]
        exp_scores = jnp.where(causal[None, None], jnp.exp(scores - norms_heads[..., None]), 0.0)
        probability = exp_scores.astype(jnp.bfloat16)
        prob_grad = jnp.einsum(
            "qkmd,wkd->kmqw", grad_four, value_block, preferred_element_type=jnp.float32
        )
        score_grad = (scale_factor * exp_scores * (prob_grad - delta_heads[..., None])).astype(
            jnp.bfloat16
        )
        query_part = jnp.einsum(
            "kmqw,wkd->qkmd", score_grad, key_block, preferred_element_type=jnp.float32
        )
        key_part = jnp.einsum(
            "kmqw,qkmd->wkd", score_grad, query_four, preferred_element_type=jnp.float32
        ).reshape(row_count, kv_width)
        value_part = jnp.einsum(
            "kmqw,qkmd->wkd", probability, grad_four, preferred_element_type=jnp.float32
        ).reshape(row_count, kv_width)
        return (query_part, jnp.concatenate([key_part, value_part], axis=1))

    query_zero = jnp.zeros((tokens, kv_local, members, HEAD_DIM), jnp.float32)

    def store_step(block_index, carry):
        query_acc, term_rows = carry
        first_row = block_index * KEY_BLOCK
        query_part, kv_part = block_terms(first_row, KEY_BLOCK)
        term_rows = lax.dynamic_update_slice_in_dim(term_rows, kv_part, first_row, 0)
        return (query_acc + query_part, term_rows)

    term_zero = jnp.zeros((length, 2 * kv_width), jnp.float32)
    query_acc, term_rows = lax.fori_loop(0, blocks_needed, store_step, (query_zero, term_zero))
    kv_sum = lax.psum_scatter(term_rows, "cp", scatter_dimension=0, tiled=True)
    query_grad = query_acc.reshape(1, tokens, kv_local * members * HEAD_DIM).astype(jnp.bfloat16)
    key_grad = kv_sum[:, :kv_width].astype(jnp.bfloat16)[None]
    value_grad = kv_sum[:, kv_width:].astype(jnp.bfloat16)[None]
    return (query_grad, key_grad, value_grad, down_grad)


def solution(mesh):
    return jax.shard_map(
        local,
        mesh=mesh,
        in_specs=(
            P("dp", "cp", "tp"),
            P("dp", "cp", "tp"),
            P("dp", "cp", "tp"),
            P("dp", "cp", "tp"),
            P("dp", "cp", "tp"),
            P("dp", "cp", "tp"),
            P("dp", "cp", "tp"),
            P("dp", "cp", None),
            P("dp", "cp", None),
            P("dp", "tp", "cp"),
        ),
        out_specs=(
            P("dp", "cp", "tp"),
            P("dp", "cp", "tp"),
            P("dp", "cp", "tp"),
            P(("cp", "dp"), "tp"),
        ),
        check_vma=False,
    )
```

profile of v0, /device:TPU:32, one launch (start us, length us, event | category | flops | bytes accessed | tf_op | source)
XLA Modules:
  0.0 598.4 jit_solution(3013731565013877724)
XLA Ops:
  7.2 0.0 copy-start
  7.2 0.0 copy-start.1
  7.2 0.0 copy-start.2
  7.2 0.0 all-gather.4.cloned.1.call-start
  7.2 1.6 copy.58
  8.9 0.0 all-gather.4.cloned.1.call-update
  8.9 0.0 all-gather.6.cloned.1.call-start
  9.0 1.6 copy.60
  10.5 0.0 all-gather.6.cloned.1.call-update
  10.6 0.0 all-gather.8.cloned.1.call-start
  10.6 0.7 all-gather.8.cloned.1.call-update
  11.3 0.0 reduce-scatter.3.cloned.1.call-start
  11.3 1.2 copy.61
  12.6 1.2 copy.62
  13.7 0.1 multiply_reduce_fusion
  13.8 0.0 copy-done.1
  13.9 0.2 copy.59
  14.1 0.0 copy-done.2
  14.1 76.5 %all-gather.4.cloned.1.call-done = bf16[1,4096,256]{1,2,0:T(8,128)(2,1)} async-done(((bf16[1,128,256]{1,2,0:T(8,128)(2,1)}), bf16[1,4096,256]{1,2,0:T(8,128)(2,1)}) %all-gather.4.cloned.1.call-update) | async-done | bytes 2097168 | tf_op jit(solution)/shard_map/all_gather | solution.py:72
  90.6 76.5 %all-gather.6.cloned.1.call-done = bf16[1,4096,256]{1,2,0:T(8,128)(2,1)} async-done(((bf16[1,128,256]{1,2,0:T(8,128)(2,1)}), bf16[1,4096,256]{1,2,0:T(8,128)(2,1)}) %all-gather.6.cloned.1.call-update) | async-done | bytes 2097168 | tf_op jit(solution)/shard_map/all_gather | solution.py:73
  167.1 1.0 broadcast_in_dim.62
  168.1 4.3 broadcast_in_dim.63.clone
  172.4 9.4 %while.13 = (s32[]{:T(128)}, f32[128,2,6,128]{0,3,2,1:T(8,128)}, f32[4096,512]{1,0:T(8,128)}, s32[]{:T(128)}, bf16[4096,2,128]{0,2,1:T(8,128)(2,1)}, /*index=5*/...) while((s32[]{:T(128)}, f32[128,2,6,128]{0,3,2,1:T(8,128)}, ...), condition=%wide.region_2.3_spmd.clone, body=%wide.region_1.0_spmd.clone.sunk | while | flops 1015808640 | bytes 25648348 | solution.py:119
  172.4 1.6 fusion.67
  173.9 0.1 broadcast_compare_fusion.3
  174.1 2.1 fusion.68
  176.2 2.6 fusion.69
  178.8 0.8 fusion.70
  179.6 0.6 fusion.71
  180.2 0.1 pad_maximum_fusion.2
  180.3 0.3 copy.92
  180.7 1.1 constant_dynamic-update-slice_fusion.2
  181.8 0.0 copy-start.3
  181.8 0.0 copy-start.4
  181.8 0.0 reduce-scatter.3.cloned.1.call-update
  181.8 0.0 reduce-scatter.5.cloned.1.call-start
  181.8 0.6 copy-done.3
  182.5 0.1 copy.66
  182.6 0.2 reduce_window_sum.11
  182.8 0.0 copy-done.4
  182.8 0.0 copy-done
  182.8 1.1 fusion.24
  183.9 0.3 copy.69
  184.3 0.5 broadcast_in_dim.70
  184.8 198.4 %all_to_all.5 = bf16[32,48,1536]{2,1,0:T(8,128)(2,1)} all-to-all(bf16[32,48,1536]{2,1,0:T(8,128)(2,1)S(1)} %bitcast.120), channel_id=1, replica_groups=mesh['cp'=32,'tp'=4,'dp'=2] {'cp'}, dimensions={0} | all-to-all | bytes 9437184 | tf_op jit(solution)/shard_map/all_to_all | solution.py:50
  383.2 0.0 all-gather.8.cloned.1.call-done
  383.2 16.1 %convolution_bitcast_fusion.1 = f32[2048,1536]{0,1:T(8,128)} fusion(bf16[1536,1536]{1,0:T(8,128)(2,1)} %bitcast.122, bf16[1,1536,2048]{2,1,0:T(8,128)(2,1)} %all-gather.8.cloned.1.call-done), kind=kOutput, calls=%fused_computation.29 | convolution fusion | flops 9663676416 | bytes 23592960 | tf_op jit(solution)/shard_map/dot_general | solution.py:52
  399.3 0.0 reduce-scatter.5.cloned.1.call-update
  399.3 1.2 convert_element_type.63
  400.5 0.9 copy.70
  401.4 33.3 %reduce-scatter.3.cloned.1.call-done = f32[128,512]{1,0:T(8,128)} async-done(((f32[4096,512]{1,0:T(8,128)}), f32[128,512]{1,0:T(8,128)}) %reduce-scatter.3.cloned.1.call-update) | async-done | bytes 262160 | tf_op jit(solution)/shard_map/reduce_scatter | solution.py:120
  434.7 1.0 convert.5
  435.7 0.7 slice_bitcast_fusion
  436.4 149.3 %reduce-scatter.5.cloned.1.call-done = f32[1024,1536]{0,1:T(8,128)} async-done(((f32[2048,1536]{0,1:T(8,128)}), f32[1024,1536]{0,1:T(8,128)}) %reduce-scatter.5.cloned.1.call-update) | async-done | bytes 6291472 | tf_op jit(solution)/shard_map/reduce_scatter | solution.py:58
  585.7 3.3 convert_element_type.69
  589.0 2.9 copy.71
  (10 shorter events, 0.1 us)
Async XLA Ops:
  7.2 175.7 %copy-start = (bf16[1,128,1536]{2,1,0:T(8,128)(2,1)S(1)}, bf16[1,128,1536]{2,1,0:T(8,128)(2,1)}, u32[]{:S(2)}) copy-start(bf16[1,128,1536]{2,1,0:T(8,128)(2,1)} %param.18) | copy-start | bytes 1179652
  7.2 6.7 %copy-start.1 = (bf16[1,128,1536]{2,1,0:T(8,128)(2,1)S(1)}, bf16[1,128,1536]{2,1,0:T(8,128)(2,1)}, u32[]{:S(2)}) copy-start(bf16[1,128,1536]{2,1,0:T(8,128)(2,1)} %param.12) | copy-start | bytes 1179652
  7.2 6.9 %copy-start.2 = (f32[1,128,12]{1,0,2:T(1,128)S(1)}, f32[1,128,12]{1,0,2:T(1,128)}, u32[]{:S(2)}) copy-start(f32[1,128,12]{1,0,2:T(1,128)} %param.17) | copy-start | bytes 18436
  7.2 83.4 %all-gather.4.cloned.1.call-start = ((), (), s32[]{:S(2)}) async-start(), calls=%async_computation.3 | async-start | bytes 2162688 | tf_op jit(solution)/shard_map/all_gather | solution.py:72
  8.9 158.2 %all-gather.6.cloned.1.call-start = ((), (), s32[]{:S(2)}) async-start(), calls=%async_computation.4 | async-start | bytes 2162688 | tf_op jit(solution)/shard_map/all_gather | solution.py:73
  10.6 372.6 %all-gather.8.cloned.1.call-start = ((), (), s32[]{:S(2)}) async-start(), calls=%async_computation.6 | async-start | bytes 7864320 | tf_op jit(solution)/shard_map/all_gather | solution.py:53
  11.3 423.4 %reduce-scatter.3.cloned.1.call-start = ((), (), s32[]{:S(2)}) async-start(), calls=%async_computation.5 | async-start | bytes 8650752 | tf_op jit(solution)/shard_map/reduce_scatter | solution.py:120
  181.8 0.7 copy-start.3
  181.8 1.0 copy-start.4
  181.8 403.9 %reduce-scatter.5.cloned.1.call-start = ((), (), s32[]{:S(2)}) async-start(), calls=%async_computation.7 | async-start | bytes 18874368 | tf_op jit(solution)/shard_map/reduce_scatter | solution.py:58
Sparse Core Ops, SparseCore 0:
  11.2 79.3 all-gather.3
  93.7 73.3 all-gather.5
  168.9 64.8 all-gather.7
  238.1 196.6 reduce-scatter.2
  437.1 148.4 reduce-scatter.4
where the time goes:
time: 601 us; the launch traced here: 598 us
  waiting for transfers between devices  336 us (56%)
  blocking collectives  198 us (33%)
  matrix products  24.9 us (4%)
  local copies, waits for them, and re-layouts  18.6 us (3%)
  between operations  13.9 us (2%)
    all_to_all x1, blocking collectives, local(): lax.all_to_all(outgoing, 'cp', split_axis=0, concat_axis=0, tiled=True)  198 us
    reduce_scatter x1, waiting for transfers between devices, local(): lax.psum_scatter(down_total, 'dp', scatter_dimension=0, tiled=True)  149 us
    all_gather x1, waiting for transfers between devices, local(): lax.all_gather(value_rows, 'cp', axis=1, tiled=True)  76.5 us
    all_gather x1, waiting for transfers between devices, local(): lax.all_gather(key_rows, 'cp', axis=1, tiled=True)  76.5 us
    reduce_scatter x1, waiting for transfers between devices, local(): kv_sum = lax.psum_scatter(term_rows, 'cp', scatter_dimension=0, tiled=True)  33.3 us
    dot_general x1, matrix products, local(): lax.dot_general(lax.all_gather(hidden_act, 'tp', axis=1, tiled=True)[0],...  16.1 us
  transfers between devices with their start and end apart: 5, of which 4 were waited for; matrix products, arithmetic and copies ran while one was open for 7% of the time, Pallas kernels for 0%

commit v1 on v0

v1 whole, which is shorter than its diff:
```python
import functools

import jax
import jax.numpy as jnp
from jax import lax
from jax.experimental import pallas as pl
from jax.experimental.pallas import tpu as pltpu
from jax.sharding import Mesh, PartitionSpec as P

HEAD_DIM = 128
MEMBERS = 6
EXPERTS = 8
CAPACITY = 48
TOKENS = 128
SCALE = HEAD_DIM ** (-0.5)
LOG2E = 1.4426950408889634
SWAP = [(0, 1), (1, 0)]
RIGHT = [(i, (i + 1) % 4) for i in range(4)]
LEFT = [(i, (i - 1) % 4) for i in range(4)]
Z = ("zq", "zl")
HALF = MEMBERS * HEAD_DIM
F32 = jnp.float32
BF16 = jnp.bfloat16


def vmem_specs(count):
    return [pl.BlockSpec(memory_space=pltpu.VMEM)] * count


def mxu(a, b, contract=((1,), (0,))):
    return lax.dot_general(a, b, (contract, ((), ())), preferred_element_type=F32)


def route_kernel(ids_ref, codes_ref, grad_ref, out_ref):
    expert = lax.broadcasted_iota(jnp.int32, (EXPERTS, TOKENS), 0)
    first = expert == ids_ref[0:1, :]
    second = expert == ids_ref[1:2, :]
    real = codes_ref[...].astype(F32) * (1.0 / 32768.0)
    hits = jnp.where(first, 1.0, 0.0) + jnp.where(second, 1.0, 0.0)
    scale = jnp.where(first, real[0:1, :], 0.0) + jnp.where(second, real[1:2, :], 0.0)
    earlier = lax.broadcasted_iota(jnp.int32, (TOKENS, TOKENS), 0)
    later = lax.broadcasted_iota(jnp.int32, (TOKENS, TOKENS), 1)
    before = jnp.where(earlier < later, 1.0, 0.0).astype(BF16)
    rank = mxu(hits.astype(BF16), before)
    rank = jnp.where(hits > 0.0, rank, -1.0)
    slot = lax.broadcasted_iota(jnp.int32, (CAPACITY, TOKENS), 0).astype(F32)
    grads = grad_ref[...]
    for e in range(EXPERTS):
        placed = rank[e : e + 1, :] == slot
        picked = mxu(jnp.where(placed, 1.0, 0.0).astype(BF16), grads)
        weight = jnp.sum(jnp.where(placed, scale[e : e + 1, :], 0.0), axis=1, keepdims=True)
        out_ref[e] = (picked * weight).astype(BF16)


def route(ids, codes, grads):
    return pl.pallas_call(
        route_kernel,
        out_shape=jax.ShapeDtypeStruct((EXPERTS, CAPACITY, grads.shape[1]), BF16),
        in_specs=vmem_specs(3),
        out_specs=vmem_specs(1)[0],
        compiler_params=pltpu.CompilerParams(vmem_limit_bytes=32 << 20),
        name="route",
    )(ids, codes, grads)


def pack_kernel(
    place_ref, query_ref, grad_ref, out_ref, norms_ref, keep_ref, send_ref, keep_rows_ref,
    send_rows_ref, delta_ref,
):
    xh = place_ref[0]
    for head in range(2 * MEMBERS):
        columns = slice(head * HEAD_DIM, (head + 1) * HEAD_DIM)
        product = grad_ref[:, columns].astype(F32) * out_ref[:, columns].astype(F32)
        delta_ref[head // MEMBERS, head % MEMBERS : head % MEMBERS + 1, :] = jnp.sum(
            product.T, axis=0, keepdims=True
        )
    for side, pack_ref, rows_ref in ((xh, keep_ref, keep_rows_ref), (1 - xh, send_ref, send_rows_ref)):
        columns = pl.ds(pl.multiple_of(side * HALF, HEAD_DIM), HALF)
        pack_ref[:, 0:HALF] = query_ref[:, columns]
        pack_ref[:, HALF : 2 * HALF] = grad_ref[:, columns]
        rows_ref[0:8, :] = norms_ref[side] * LOG2E
        rows_ref[8:16, :] = delta_ref[side]


def pack(xh, query, grad, out, norms):
    width = query.shape[1]
    shape = jax.ShapeDtypeStruct((TOKENS, width), BF16)
    rows = jax.ShapeDtypeStruct((16, TOKENS), F32)
    return pl.pallas_call(
        pack_kernel,
        out_shape=(shape, shape, rows, rows),
        in_specs=[pl.BlockSpec(memory_space=pltpu.SMEM)] + vmem_specs(4),
        out_specs=tuple(vmem_specs(4)),
        scratch_shapes=[pltpu.VMEM((2, 8, TOKENS), F32)],
        compiler_params=pltpu.CompilerParams(vmem_limit_bytes=32 << 20),
        name="pack",
    )(xh[None], query, grad, out, norms)


def attention_kernel(
    place_ref, kv_ref, p00, p01, p10, p11, r00, r01, r10, r11,
    dkv_ref, keep_ref, send_ref,
    q_ref, do_ref, qt_ref, dot_ref, dqt_ref, rows_ref, diff_ref, acc_ref,
):
    xh, z, co = place_ref[0], place_ref[1], place_ref[2]
    packs = ((p00, p01), (p10, p11))
    rows = ((r00, r01), (r10, r11))
    for g in range(2):
        for c in range(2):
            span = slice(c * TOKENS, (c + 1) * TOKENS)
            rows_ref[g, :, span] = rows[g][c][...]
            for h in range(MEMBERS):
                block = packs[g][c][:, h * HEAD_DIM : (h + 1) * HEAD_DIM]
                q_ref[g, h, span, :] = block
                qt_ref[g, h, :, span] = block.T
                block = packs[g][c][:, HALF + h * HEAD_DIM : HALF + (h + 1) * HEAD_DIM]
                do_ref[g, h, span, :] = block
                dot_ref[g, h, :, span] = block.T
    dqt_ref[...] = jnp.zeros_like(dqt_ref)
    key_row = lax.broadcasted_iota(jnp.int32, (256, 256), 0)
    query_row = lax.broadcasted_iota(jnp.int32, (256, 256), 1)
    own = query_row < TOKENS
    query_at = jnp.where(own, query_row + co * TOKENS, query_row - TOKENS + (1 - co) * TOKENS)
    diff_ref[...] = query_at - jnp.where(key_row < TOKENS, key_row, key_row + TOKENS)

    def chunk(index, _):
        slot, t = index // 4, index % 4
        xh_key = jnp.where(slot == 0, xh, 1 - xh)
        kv = kv_ref[pl.ds(2 * t, 2), slot].reshape(256, 256)
        key, value = kv[:, :HEAD_DIM], kv[:, HEAD_DIM:]
        key_t = key.T
        acc_ref[...] = jnp.zeros_like(acc_ref)
        for g in range(2):
            xh_query = xh if g == 0 else 1 - xh
            seen = (xh_key < xh_query) | ((xh_key == xh_query) & (t <= z // 2))
            bound = (xh_key - xh_query) * 2048 + t * 512 + co * TOKENS - z * 256

            @pl.when(seen)
            def _():
                key_part = jnp.zeros((256, HEAD_DIM), F32)
                value_part = jnp.zeros((256, HEAD_DIM), F32)
                for h in range(MEMBERS):
                    scores = mxu(key, qt_ref[g, h])
                    exp_scores = jnp.exp2(scores * (SCALE * LOG2E) - rows_ref[g, h : h + 1, :])
                    exp_scores = jnp.where(diff_ref[...] >= bound, exp_scores, 0.0)
                    prob_grad = mxu(value, dot_ref[g, h])
                    value_part += mxu(exp_scores.astype(BF16), do_ref[g, h])
                    score_grad = (
                        (SCALE * exp_scores) * (prob_grad - rows_ref[g, 8 + h : 9 + h, :])
                    ).astype(BF16)
                    key_part += mxu(score_grad, q_ref[g, h])
                    dqt_ref[g, h] += mxu(key_t, score_grad)
                acc_ref[:, :HEAD_DIM] += key_part
                acc_ref[:, HEAD_DIM:] += value_part

        dkv_ref[pl.ds(2 * t, 2), slot] = acc_ref[...].astype(BF16).reshape(2, TOKENS, 256)
        return 0

    lax.fori_loop(0, 8, chunk, 0)
    for g in range(2):
        for h in range(MEMBERS):
            columns = slice(h * HEAD_DIM, (h + 1) * HEAD_DIM)
            total = dqt_ref[g, h]
            keep_ref[g, :, columns] = total[:, :TOKENS].T
            send_ref[g, :, columns] = total[:, TOKENS:].T.astype(BF16)


def attention(place, kv, packs, rows):
    return pl.pallas_call(
        attention_kernel,
        out_shape=(
            jax.ShapeDtypeStruct(kv.shape, BF16),
            jax.ShapeDtypeStruct((2, TOKENS, HALF), F32),
            jax.ShapeDtypeStruct((2, TOKENS, HALF), BF16),
        ),
        in_specs=[pl.BlockSpec(memory_space=pltpu.SMEM)] + vmem_specs(9),
        out_specs=tuple(vmem_specs(3)),
        scratch_shapes=[
            pltpu.VMEM((2, MEMBERS, 256, HEAD_DIM), BF16),
            pltpu.VMEM((2, MEMBERS, 256, HEAD_DIM), BF16),
            pltpu.VMEM((2, MEMBERS, HEAD_DIM, 256), BF16),
            pltpu.VMEM((2, MEMBERS, HEAD_DIM, 256), BF16),
            pltpu.VMEM((2, MEMBERS, HEAD_DIM, 256), F32),
            pltpu.VMEM((2, 16, 256), F32),
            pltpu.VMEM((256, 256), jnp.int32),
            pltpu.VMEM((256, 256), F32),
        ],
        compiler_params=pltpu.CompilerParams(vmem_limit_bytes=48 << 20),
        name="attention",
    )(place, kv, *packs, *rows)


def down_kernel(place_ref, *refs):
    routed = refs[0:4]
    hidden = refs[4:14]
    out_ref, gathered_ref = refs[14], refs[15]
    dp, tp = place_ref[0], place_ref[1]

    @pl.when(pl.program_id(0) == 0)
    def _():
        for s in range(2):
            seq = dp if s == 0 else 1 - dp
            own, left, right, far_low, far_high = hidden[5 * s : 5 * s + 5]
            here = seq * 4 + tp
            before = seq * 4 + lax.rem(tp + 3, 4)
            after = seq * 4 + lax.rem(tp + 1, 4)
            far = seq * 4 + lax.rem(tp + 2, 4)
            for m in range(4):
                gathered_ref[m, here] = own[m]
                gathered_ref[m, before] = left[m]
                gathered_ref[m, after] = right[m]
                gathered_ref[m, far] = far_low[m] if m < 2 else far_high[m - 2]

    total = None
    for m in range(4):
        left = gathered_ref[m].reshape(768, gathered_ref.shape[3])
        right = routed[m][...].reshape(768, out_ref.shape[1])
        part = mxu(left, right, ((0,), (0,)))
        total = part if total is None else total + part
    out_ref[...] = total.astype(BF16)


def down(place, routed, hidden, tile=512):
    width = routed.shape[-1]
    rows = hidden[0].shape[-1]
    whole = lambda i, p: (0, 0, 0)
    return pl.pallas_call(
        down_kernel,
        grid_spec=pltpu.PrefetchScalarGridSpec(
            num_scalar_prefetch=1,
            grid=(width // tile,),
            in_specs=[
                pl.BlockSpec((None, 8, 96, tile), functools.partial(lambda m, i, p: (m, 0, 0, i), m))
                for m in range(4)
            ]
            + [pl.BlockSpec(h.shape, whole, pipeline_mode=pl.Buffered(1)) for h in hidden],
            out_specs=pl.BlockSpec((rows, tile), lambda i, p: (0, i)),
            scratch_shapes=[pltpu.VMEM((4, 8, 96, rows), BF16)],
        ),
        out_shape=jax.ShapeDtypeStruct((rows, width), BF16),
        compiler_params=pltpu.CompilerParams(vmem_limit_bytes=56 << 20),
        name="down",
    )(place, routed, routed, routed, routed, *hidden)


def local(
    query_rows,
    key_rows,
    value_rows,
    attention_out,
    output_grad,
    log_norms,
    moe_grad,
    expert_ids,
    route_weight,
    hidden_act,
):
    xh, co, dp, tp = (lax.axis_index(name) for name in ("xh", "co", "dp", "tp"))
    z = lax.axis_index(Z)

    def by_side(array, side):
        return lax.dynamic_index_in_dim(array, side, 0, keepdims=False)

    kv = jnp.concatenate(
        [key_rows[0].reshape(TOKENS, 2, HEAD_DIM), value_rows[0].reshape(TOKENS, 2, HEAD_DIM)],
        axis=2,
    ).transpose(1, 0, 2)
    kv_other = lax.ppermute(by_side(kv, 1 - xh), "xh", SWAP)
    kv_all = lax.all_gather(jnp.stack([by_side(kv, xh), kv_other]), Z, axis=0)

    hidden = hidden_act[0].reshape(2, 4, CAPACITY, 2, 1024).transpose(3, 1, 0, 2, 4)
    hidden = hidden.reshape(2, 4, 2 * CAPACITY, 1024)
    hidden_own = by_side(hidden, dp)
    hidden_other = lax.ppermute(by_side(hidden, 1 - dp), "dp", SWAP)

    routed = route(expert_ids[0].T, route_weight[0].T, moe_grad[0])
    arrived = lax.all_to_all(routed, ("xh", "zq"), 0, 0, tiled=True)
    arrived = lax.all_gather(arrived, ("zl", "co", "dp"), axis=0)
    arrived = arrived.reshape(4, 8, 2 * CAPACITY, moe_grad.shape[2])

    pieces = []
    for piece in (hidden_own, hidden_other):
        left = lax.ppermute(piece, "tp", RIGHT)
        right = lax.ppermute(piece, "tp", LEFT)
        far_low = lax.ppermute(left[:2], "tp", RIGHT)
        far_high = lax.ppermute(right[2:], "tp", LEFT)
        pieces += [piece, left, right, far_low, far_high]

    norms = jnp.pad(log_norms[0].T.reshape(2, MEMBERS, TOKENS), ((0, 0), (0, 2), (0, 0)))
    keep, send, keep_rows, send_rows = pack(
        xh, query_rows[0], output_grad[0], attention_out[0], norms
    )
    across = lax.ppermute(send, "xh", SWAP)
    across_rows = lax.ppermute(send_rows, "xh", SWAP)
    packs = (keep, lax.ppermute(keep, "co", SWAP), across, lax.ppermute(across, "co", SWAP))
    rows_near = lax.ppermute(jnp.stack([keep_rows, across_rows]), "co", SWAP)
    rows = (keep_rows, rows_near[0], across_rows, rows_near[1])
    dkv, dq_keep, dq_send = attention(jnp.stack([xh, z, co]), kv_all, packs, rows)

    dq = (dq_keep + lax.ppermute(dq_send, "co", SWAP).astype(F32)).astype(BF16)
    dq_across = lax.ppermute(dq[1], "xh", SWAP)
    dkv = jnp.sum(lax.all_to_all(dkv, Z, 0, 0, tiled=True).astype(F32), axis=0).astype(BF16)
    dkv_across = lax.ppermute(dkv[1], "xh", SWAP)

    def in_order(mine, other):
        low = jnp.where(xh == 0, mine, other)
        high = jnp.where(xh == 0, other, mine)
        return low, high

    query_grad = jnp.concatenate(in_order(dq[0], dq_across), axis=1)[None]
    low, high = in_order(dkv[0], dkv_across)
    key_grad = jnp.concatenate([low[:, :HEAD_DIM], high[:, :HEAD_DIM]], axis=1)[None]
    value_grad = jnp.concatenate([low[:, HEAD_DIM:], high[:, HEAD_DIM:]], axis=1)[None]
    down_grad = down(jnp.stack([dp, tp]), arrived, pieces)
    return (query_grad, key_grad, value_grad, down_grad)


def solution(mesh):
    fine = Mesh(mesh.devices.reshape(2, 4, 2, 2, 4, 2), ("xh", "zq", "zl", "co", "tp", "dp"))
    cp = ("xh", "zq", "zl", "co")
    return jax.shard_map(
        local,
        mesh=fine,
        in_specs=(
            P("dp", cp, "tp"),
            P("dp", cp, "tp"),
            P("dp", cp, "tp"),
            P("dp", cp, "tp"),
            P("dp", cp, "tp"),
            P("dp", cp, "tp"),
            P("dp", cp, "tp"),
            P("dp", cp, None),
            P("dp", cp, None),
            P("dp", "tp", cp),
        ),
        out_specs=(
            P("dp", cp, "tp"),
            P("dp", cp, "tp"),
            P("dp", cp, "tp"),
            P(cp + ("dp",), "tp"),
        ),
        check_vma=False,
    )
```

time: 601 us -> 193 us (0.32)
  waiting for transfers between devices: 336 us -> 72.8 us
  blocking collectives: 198 us -> 0 us
  starting transfers between devices: 0.2 us -> 51.2 us
  Pallas kernels: 0 us -> 31 us
  matrix products: 24.9 us -> 0 us
    all_to_all x1 -> x0, blocking collectives: 198 us -> none  [local(): lax.all_to_all(outgoing, 'cp', split_axis=0, concat_axis=0, tiled=True)]
    reduce_scatter x2 -> x0, waiting for transfers between devices: 183 us -> none  [the longest x1 149 us: local(): lax.psum_scatter(down_total, 'dp', scatter_dimension=0, tiled=True)]
    all_gather x3 -> x2, waiting for transfers between devices: 153 us -> 1.72 us  [the longest x1 1.7 us: local(): kv_all = lax.all_gather(jnp.stack([by_side(kv, xh), kv_other]), Z, axis=0)]
    ppermute x0 -> x18, waiting for transfers between devices: none -> 46.3 us  [the longest x1 22.2 us: local(): hidden_other = lax.ppermute(by_side(hidden, 1 - dp), 'dp', SWAP)]
    pallas_call x0 -> x4, Pallas kernels: none -> 31 us  [the longest x1 16.4 us: down(): pl.pallas_call(down_kernel, grid_spec=pltpu.PrefetchScalarGridSpec(num_sc...]
    ppermute x0 -> x18, starting transfers between devices: none -> 26.8 us  [the longest x2 5.38 us: local(): far_high = lax.ppermute(right[2:], 'tp', LEFT)]
    dot_general x7 -> x0, matrix products: 24.9 us -> none  [the longest x1 16.1 us: local(): lax.dot_general(lax.all_gather(hidden_act, 'tp', axis=1, tiled=True)[0],...]
    all_to_all x0 -> x2, waiting for transfers between devices: none -> 24.7 us  [the longest x1 24.7 us: local(): arrived = lax.all_to_all(routed, ('xh', 'zq'), 0, 0, tiled=True)]
  transfers between devices with their start and end apart: 5 -> 22, of which waited for: 4 -> 8; matrix products, arithmetic and copies ran while one was open for 7% -> 9% of each run, Pallas kernels for 0% -> 7%
where the time goes in v1:
time: 193 us
  waiting for transfers between devices  72.8 us (38%)
  starting transfers between devices  51.2 us (27%)
  Pallas kernels  31 us (16%)
  local copies, waits for them, and re-layouts  17.6 us (9%)
  between operations  14.3 us (7%)
  other arithmetic  5.83 us (3%)
    all_to_all x1, waiting for transfers between devices, local(): arrived = lax.all_to_all(routed, ('xh', 'zq'), 0, 0, tiled=True)  24.7 us
    ppermute x1, waiting for transfers between devices, local(): hidden_other = lax.ppermute(by_side(hidden, 1 - dp), 'dp', SWAP)  22.2 us
    pallas_call x1, Pallas kernels, down(): pl.pallas_call(down_kernel, grid_spec=pltpu.PrefetchScalarGridSpec(num_sc...  16.4 us
    all_to_all x1, starting transfers between devices, local(): lax.all_to_all(dkv, Z, 0, 0, tiled=True).astype(F32)  14.2 us
    pallas_call x1, Pallas kernels, attention(): pl.pallas_call(attention_kernel, out_shape=(jax.ShapeDtypeStruct(kv.shape...  12.6 us
    all_to_all x1, starting transfers between devices, local(): arrived = lax.all_to_all(routed, ('xh', 'zq'), 0, 0, tiled=True)  10.2 us
    ppermute x2, waiting for transfers between devices, local(): left = lax.ppermute(piece, 'tp', RIGHT)  9.74 us
    ppermute x1, waiting for transfers between devices, local(): across = lax.ppermute(send, 'xh', SWAP)  7.35 us
  transfers between devices with their start and end apart: 22, of which 8 were waited for; matrix products, arithmetic and copies ran while one was open for 9% of the time, Pallas kernels for 7%

profile of v1, /device:TPU:32, one launch (start us, length us, event | category | flops | bytes accessed | tf_op | source)
XLA Modules:
  0.0 192.8 jit_solution(2354547080565706846)
XLA Ops:
  7.2 1.0 copy-done.1
  8.2 0.7 copy-done.5
  8.8 0.7 copy-done.6
  9.5 1.7 route.1
  11.2 10.2 %all-to-all-start.1 = ((bf16[8,48,1536]{2,1,0:T(8,128)(2,1)}), bf16[8,48,1536]{2,1,0:T(8,128)(2,1)S(1)}, u32[]{:S(2)}, u32[]{:S(2)}) async-start(bf16[8,48,1536]{2,1,0:T(8,128)(2,1)} %route.1), calls=%async_computation.1 | async-start | bytes 2359296 | tf_op jit(solution)/shard_map/all_to_all | solution.py:277
  21.4 0.0 all-gather.5.cloned.1.call-start
  21.5 0.1 copy.21
  21.6 0.1 copy.22
  21.8 0.1 copy.24
  21.9 3.6 %collective-permute-start = (bf16[128,256]{1,0:T(8,128)(2,1)S(1)}, bf16[128,256]{1,0:T(8,128)(2,1)S(1)}, u32[]{:S(2)}, u32[]{:S(2)}) collective-permute-start(bf16[128,256]{1,0:T(8,128)(2,1)S(1)} %bitcast.79), channel_id=1, source_target_pairs={{0,128},{128,0},{1,129},{129,1},{2,130},{130,2},{3,131},{131,3},{4... | collective-permute-start | bytes 196616 | tf_op jit(solution)/shard_map/ppermute | solution.py:268
  25.5 0.1 copy.23
  25.6 4.7 %collective-permute-done = bf16[128,256]{1,0:T(8,128)(2,1)S(1)} collective-permute-done((bf16[128,256]{1,0:T(8,128)(2,1)S(1)}, bf16[128,256]{1,0:T(8,128)(2,1)S(1)}, u32[]{:S(2)}, u32[]{:S(2)}) %collective-permute-start) | collective-permute-done | bytes 65568 | tf_op jit(solution)/shard_map/ppermute | solution.py:268
  30.3 0.7 pad_maximum_fusion
  30.9 0.0 all-gather.5.cloned.1.call-update
  30.9 0.0 all-gather.7.cloned.1.call-start
  31.0 24.7 %all-to-all-done.1 = bf16[8,48,1536]{2,1,0:T(8,128)(2,1)S(1)} async-done(((bf16[8,48,1536]{2,1,0:T(8,128)(2,1)}), bf16[8,48,1536]{2,1,0:T(8,128)(2,1)S(1)}, u32[]{:S(2)}, u32[]{:S(2)}) %all-to-all-start.1) | async-done | bytes 1179680 | tf_op jit(solution)/shard_map/all_to_all | solution.py:277
  55.7 1.0 copy-done.8
  56.7 0.0 all-gather.7.cloned.1.call-update
  56.8 0.3 pack.1
  57.1 0.1 collective-permute-start.2
  57.2 3.5 %collective-permute-start.4 = (f32[16,128]{1,0:T(8,128)S(1)}, f32[16,128]{1,0:T(8,128)S(1)}, u32[]{:S(2)}, u32[]{:S(2)}) collective-permute-start(f32[16,128]{1,0:T(8,128)S(1)} %get-tuple-element.14), channel_id=1, source_target_pairs={{0,128},{128,0},{1,129},{129,1},{2,130},{130,2},{3,131},{131,3},{4... | collective-permute-start | bytes 24584 | tf_op jit(solution)/shard_map/ppermute | solution.py:294
  60.7 7.3 %collective-permute-done.2.p10 = bf16[128,1536]{1,0:T(8,128)(2,1)S(1)} collective-permute-done((bf16[128,1536]{1,0:T(8,128)(2,1)S(1)}, bf16[128,1536]{1,0:T(8,128)(2,1)S(1)}, u32[]{:S(2)}, u32[]{:S(2)}) %collective-permute-start.2) | collective-permute-done | bytes 393248 | tf_op jit(solution)/shard_map/ppermute | solution.py:293
  68.1 0.1 collective-permute-done.4.r10
  68.2 0.4 collective-permute-start.5
  68.6 0.1 pad_add_fusion.place_ref
  68.7 2.9 %reshape_squeeze.11 = bf16[2,4,48,2,1024]{4,3,2,1,0:T(2,128)(2,1)S(1)} reshape(bf16[1,384,2048]{2,1,0:T(8,128)(2,1)} %param.19) | data formatting | bytes 3145728 | tf_op jit(solution)/shard_map/reshape;squeeze | solution.py:271
  71.6 1.6 copy.25
  73.2 1.7 all-gather.5.cloned.1.call-done
  74.9 1.2 copy-done
  76.1 12.6 %attention.1 = (bf16[8,2,128,256]{3,2,1,0:T(8,128)(2,1)}, f32[2,128,768]{2,1,0:T(8,128)S(1)}, bf16[2,128,768]{2,1,0:T(8,128)(2,1)S(1)}) custom-call(s32[3]{0:T(128)S(1)} %pad_add_fusion.place_ref, bf16[8,2,128,256]{3,2,1,0:T(8,128)(2,1)S(1)} %bitcast.61, bf16[128,1536]{1,0:T(8,128)(2,1)S(1)} %get-tuple-element.11.p00, ...), custom_call_target="tpu_custom_call" | custom-call | tf_op jit(solution)/shard_map/attention/pallas_call | solution.py:169
  88.7 14.2 %all-to-all-start = ((bf16[8,2,128,256]{3,2,1,0:T(8,128)(2,1)}), bf16[8,2,128,256]{3,2,1,0:T(8,128)(2,1)}, u32[]{:S(2)}, u32[]{:S(2)}) async-start(bf16[8,2,128,256]{3,2,1,0:T(8,128)(2,1)} %get-tuple-element.17), calls=%async_computation | async-start | bytes 2097152 | tf_op jit(solution)/shard_map/all_to_all | solution.py:302
  102.9 1.1 dynamic-slice_bitcast_fusion
  104.0 0.6 collective-permute-start.13
  104.6 1.5 collective-permute-start.9
  106.1 1.7 collective-permute-start.10
  107.8 22.2 %collective-permute-done.13.refs_9_ = bf16[4,96,1024]{2,1,0:T(8,128)(2,1)} collective-permute-done((bf16[4,96,1024]{2,1,0:T(8,128)(2,1)S(1)}, bf16[4,96,1024]{2,1,0:T(8,128)(2,1)}, u32[]{:S(2)}, u32[]{:S(2)}) %collective-permute-start.13) | collective-permute-done | bytes 786464 | tf_op jit(solution)/shard_map/ppermute | solution.py:274
  130.0 1.5 collective-permute-start.14
  131.5 1.8 collective-permute-start.15
  133.3 0.1 add_convert_fusion
  133.4 0.7 slice_bitcast_fusion
  134.0 2.8 %collective-permute-start.7 = (bf16[128,768]{1,0:T(8,128)(2,1)}, bf16[128,768]{1,0:T(8,128)(2,1)}, u32[]{:S(2)}, u32[]{:S(2)}) collective-permute-start(bf16[128,768]{1,0:T(8,128)(2,1)} %slice_bitcast_fusion), channel_id=1, source_target_pairs={{0,128},{128,0},{1,129},{129,1},{2,130},{130,2},{3,131},{131,3},{4... | collective-permute-start | bytes 589832 | tf_op jit(solution)/shard_map/ppermute | solution.py:301
  136.8 0.6 pad_add_fusion.1.place_ref
  137.4 0.8 slice.66
  138.2 0.8 collective-permute-start.11
  139.1 0.8 slice.67
  139.9 2.4 %collective-permute-start.12 = (bf16[2,96,1024]{2,1,0:T(8,128)(2,1)}, bf16[2,96,1024]{2,1,0:T(8,128)(2,1)S(1)}, u32[]{:S(2)}, u32[]{:S(2)}) collective-permute-start(bf16[2,96,1024]{2,1,0:T(8,128)(2,1)} %slice.67), channel_id=1, source_target_pairs={{0,6},{2,0},{4,2},{6,4},{1,7},{3,1},{5,3},{7,5},{8,14},{10,8},{12,... | collective-permute-start | bytes 1179656 | tf_op jit(solution)/shard_map/ppermute | solution.py:286
  142.3 9.7 %collective-permute-done.14.refs_10_ = bf16[4,96,1024]{2,1,0:T(8,128)(2,1)} collective-permute-done((bf16[4,96,1024]{2,1,0:T(8,128)(2,1)}, bf16[4,96,1024]{2,1,0:T(8,128)(2,1)}, u32[]{:S(2)}, u32[]{:S(2)}) %collective-permute-start.14) | collective-permute-done | bytes 786464 | tf_op jit(solution)/shard_map/ppermute | solution.py:283
  152.0 1.8 slice.68
  153.8 0.2 collective-permute-start.16
  154.0 1.8 slice.69
  155.8 3.0 %collective-permute-start.17 = (bf16[2,96,1024]{2,1,0:T(8,128)(2,1)}, bf16[2,96,1024]{2,1,0:T(8,128)(2,1)S(1)}, u32[]{:S(2)}, u32[]{:S(2)}) collective-permute-start(bf16[2,96,1024]{2,1,0:T(8,128)(2,1)} %slice.69), channel_id=1, source_target_pairs={{0,6},{2,0},{4,2},{6,4},{1,7},{3,1},{5,3},{7,5},{8,14},{10,8},{12,... | collective-permute-start | bytes 1179656 | tf_op jit(solution)/shard_map/ppermute | solution.py:286
  158.8 1.0 broadcast_select_fusion.1
  159.8 1.4 reduce_sum.12
  161.2 2.9 %collective-permute-start.8 = (bf16[128,256]{1,0:T(8,128)(2,1)S(1)}, bf16[128,256]{1,0:T(8,128)(2,1)S(1)}, u32[]{:S(2)}, u32[]{:S(2)}) collective-permute-start(bf16[128,256]{1,0:T(8,128)(2,1)S(1)} %slice_bitcast_fusion.2), channel_id=1, source_target_pairs={{0,128},{128,0},{1,129},{129,1},{2,130},{130,2},{3,131},{131,3},{4... | collective-permute-start | bytes 196616 | tf_op jit(solution)/shard_map/ppermute | solution.py:303
  164.0 0.8 maximum_bitcast_fusion
  164.8 2.2 %collective-permute-done.8 = bf16[128,256]{1,0:T(8,128)(2,1)S(1)} collective-permute-done((bf16[128,256]{1,0:T(8,128)(2,1)S(1)}, bf16[128,256]{1,0:T(8,128)(2,1)S(1)}, u32[]{:S(2)}, u32[]{:S(2)}) %collective-permute-start.8) | collective-permute-done | bytes 65568 | tf_op jit(solution)/shard_map/ppermute | solution.py:303
  167.1 0.6 maximum_bitcast_fusion.2
  167.7 0.6 maximum_bitcast_fusion.1
  168.4 0.0 all-gather.7.cloned.1.call-done
  168.5 0.7 copy-done.11
  169.1 0.1 copy-done.12
  169.2 0.1 copy-done.13
  169.4 0.1 copy-done.14
  169.5 16.4 %down.1 = bf16[1024,1536]{1,0:T(8,128)(2,1)} custom-call(s32[2]{0:T(128)} %pad_add_fusion.1.place_ref, bf16[4,8,96,1536]{3,2,1,0:T(8,128)(2,1)} %bitcast.70, bf16[4,8,96,1536]{3,2,1,0:T(8,128)(2,1)} %bitcast.71, bf16[4,8,96,1536]{3,2,1,0:T(8,128)(2,1)} %bitcast.72, bf16[4,8,96,1536]{3,2,1,0:T(8,128)(2,1)} %bitcast.73, ...), custom_call_target="tpu_custom_call" | custom-call | tf_op jit(solution)/shard_map/down/pallas_call | solution.py:227
  (52 shorter events, 0.2 us)
Async XLA Ops:
  7.2 1.0 copy-start.1
  8.2 0.7 copy-start.5
  8.8 0.7 copy-start.6
  11.2 10.3 %copy-start.15 = (bf16[1,128,256]{2,1,0:T(8,128)(2,1)S(1)}, bf16[1,128,256]{2,1,0:T(8,128)(2,1)}, u32[]{:S(2)}) copy-start(bf16[1,128,256]{2,1,0:T(8,128)(2,1)} %param.11) | copy-start | bytes 196612
  11.2 10.4 %copy-start.16 = (bf16[1,128,256]{2,1,0:T(8,128)(2,1)S(1)}, bf16[1,128,256]{2,1,0:T(8,128)(2,1)}, u32[]{:S(2)}) copy-start(bf16[1,128,256]{2,1,0:T(8,128)(2,1)} %param.12) | copy-start | bytes 196612
  11.2 44.5 %all-to-all-start.1 = ((bf16[8,48,1536]{2,1,0:T(8,128)(2,1)}), bf16[8,48,1536]{2,1,0:T(8,128)(2,1)S(1)}, u32[]{:S(2)}, u32[]{:S(2)}) async-start(bf16[8,48,1536]{2,1,0:T(8,128)(2,1)} %route.1), calls=%async_computation.1 | async-start | bytes 2359296 | tf_op jit(solution)/shard_map/all_to_all | solution.py:277
  21.4 35.4 %copy-start.17 = (f32[1,128,12]{1,0,2:T(1,128)S(1)}, f32[1,128,12]{1,0,2:T(1,128)}, u32[]{:S(2)}) copy-start(f32[1,128,12]{1,0,2:T(1,128)} %param.15) | copy-start | bytes 18436
  21.4 35.4 %copy-start.2 = (bf16[1,128,1536]{2,1,0:T(8,128)(2,1)S(1)}, bf16[1,128,1536]{2,1,0:T(8,128)(2,1)}, u32[]{:S(2)}) copy-start(bf16[1,128,1536]{2,1,0:T(8,128)(2,1)} %param.10) | copy-start | bytes 1179652
  21.4 35.4 %copy-start.3 = (bf16[1,128,1536]{2,1,0:T(8,128)(2,1)S(1)}, bf16[1,128,1536]{2,1,0:T(8,128)(2,1)}, u32[]{:S(2)}) copy-start(bf16[1,128,1536]{2,1,0:T(8,128)(2,1)} %param.14) | copy-start | bytes 1179652
  21.4 35.4 %copy-start.4 = (bf16[1,128,1536]{2,1,0:T(8,128)(2,1)S(1)}, bf16[1,128,1536]{2,1,0:T(8,128)(2,1)}, u32[]{:S(2)}) copy-start(bf16[1,128,1536]{2,1,0:T(8,128)(2,1)} %param.13) | copy-start | bytes 1179652
  21.4 53.5 %all-gather.5.cloned.1.call-start = ((), (), s32[]{:S(2)}) async-start(), calls=%async_computation.2 | async-start | bytes 1179648 | tf_op jit(solution)/shard_map/all_gather | solution.py:269
  21.9 8.4 %collective-permute-start = (bf16[128,256]{1,0:T(8,128)(2,1)S(1)}, bf16[128,256]{1,0:T(8,128)(2,1)S(1)}, u32[]{:S(2)}, u32[]{:S(2)}) collective-permute-start(bf16[128,256]{1,0:T(8,128)(2,1)S(1)} %bitcast.79), channel_id=1, source_target_pairs={{0,128},{128,0},{1,129},{129,1},{2,130},{130,2},{3,131},{131,3},{4... | collective-permute-start | bytes 196616 | tf_op jit(solution)/shard_map/ppermute | solution.py:268
  30.9 137.5 %all-gather.7.cloned.1.call-start = ((), (), s32[]{:S(2)}) async-start(), calls=%async_computation.3 | async-start | bytes 10616832 | tf_op jit(solution)/shard_map/all_gather | solution.py:278
  55.7 1.0 copy-start.8
  57.1 11.0 %collective-permute-start.2 = (bf16[128,1536]{1,0:T(8,128)(2,1)S(1)}, bf16[128,1536]{1,0:T(8,128)(2,1)S(1)}, u32[]{:S(2)}, u32[]{:S(2)}) collective-permute-start(bf16[128,1536]{1,0:T(8,128)(2,1)S(1)} %get-tuple-element.12), channel_id=1, source_target_pairs={{0,128},{128,0},{1,129},{129,1},{2,130},{130,2},{3,131},{131,3},{4... | collective-permute-start | bytes 1179656 | tf_op jit(solution)/shard_map/ppermute | solution.py:293
  57.2 11.0 %collective-permute-start.4 = (f32[16,128]{1,0:T(8,128)S(1)}, f32[16,128]{1,0:T(8,128)S(1)}, u32[]{:S(2)}, u32[]{:S(2)}) collective-permute-start(f32[16,128]{1,0:T(8,128)S(1)} %get-tuple-element.14), channel_id=1, source_target_pairs={{0,128},{128,0},{1,129},{129,1},{2,130},{130,2},{3,131},{131,3},{4... | collective-permute-start | bytes 24584 | tf_op jit(solution)/shard_map/ppermute | solution.py:294
  60.7 12.4 %collective-permute-start.1 = (bf16[128,1536]{1,0:T(8,128)(2,1)S(1)}, bf16[128,1536]{1,0:T(8,128)(2,1)S(1)}, u32[]{:S(2)}, u32[]{:S(2)}) collective-permute-start(bf16[128,1536]{1,0:T(8,128)(2,1)S(1)} %get-tuple-element.11.p00), channel_id=1, source_target_pairs={{0,8},{8,0},{1,9},{9,1},{2,10},{10,2},{3,11},{11,3},{4,12},{12,4},... | collective-permute-start | bytes 1179656 | tf_op jit(solution)/shard_map/ppermute | solution.py:295
  68.1 5.1 %collective-permute-start.3 = (bf16[128,1536]{1,0:T(8,128)(2,1)S(1)}, bf16[128,1536]{1,0:T(8,128)(2,1)S(1)}, u32[]{:S(2)}, u32[]{:S(2)}) collective-permute-start(bf16[128,1536]{1,0:T(8,128)(2,1)S(1)} %collective-permute-done.2.p10), channel_id=1, source_target_pairs={{0,8},{8,0},{1,9},{9,1},{2,10},{10,2},{3,11},{11,3},{4,12},{12,4},... | collective-permute-start | bytes 1179656 | tf_op jit(solution)/shard_map/ppermute | solution.py:295
  68.2 5.0 %collective-permute-start.5 = (f32[2,16,128]{2,1,0:T(8,128)S(1)}, f32[2,16,128]{2,1,0:T(8,128)S(1)}, u32[]{:S(2)}, u32[]{:S(2)}) collective-permute-start(f32[2,16,128]{2,1,0:T(8,128)S(1)} %pad_maximum_fusion.1), channel_id=1, source_target_pairs={{0,8},{8,0},{1,9},{9,1},{2,10},{10,2},{3,11},{11,3},{4,12},{12,4},... | collective-permute-start | bytes 49160 | tf_op jit(solution)/shard_map/ppermute | solution.py:296
  74.9 1.2 copy-start
  88.7 14.2 %copy-start.7 = (bf16[2,4,2,48,1024]{4,3,2,1,0:T(8,128)(2,1)S(1)}, bf16[2,4,2,48,1024]{4,3,2,1,0:T(8,128)(2,1)}, u32[]{:S(2)}) copy-start(bf16[2,4,2,48,1024]{4,3,2,1,0:T(8,128)(2,1)} %copy.25) | copy-start | bytes 4718596
  88.7 71.1 %all-to-all-start = ((bf16[8,2,128,256]{3,2,1,0:T(8,128)(2,1)}), bf16[8,2,128,256]{3,2,1,0:T(8,128)(2,1)}, u32[]{:S(2)}, u32[]{:S(2)}) async-start(bf16[8,2,128,256]{3,2,1,0:T(8,128)(2,1)} %get-tuple-element.17), calls=%async_computation | async-start | bytes 2097152 | tf_op jit(solution)/shard_map/all_to_all | solution.py:302
  104.0 26.0 %collective-permute-start.13 = (bf16[4,96,1024]{2,1,0:T(8,128)(2,1)S(1)}, bf16[4,96,1024]{2,1,0:T(8,128)(2,1)}, u32[]{:S(2)}, u32[]{:S(2)}) collective-permute-start(bf16[4,96,1024]{2,1,0:T(8,128)(2,1)S(1)} %get-tuple-element.18), channel_id=1, source_target_pairs={{0,1},{1,0},{2,3},{3,2},{4,5},{5,4},{6,7},{7,6},{8,9},{9,8},{10,11... | collective-permute-start | bytes 2359304 | tf_op jit(solution)/shard_map/ppermute | solution.py:274
  104.5 28.7 %collective-permute-start.6 = (bf16[2,128,768]{2,1,0:T(8,128)(2,1)S(1)}, bf16[2,128,768]{2,1,0:T(8,128)(2,1)S(1)}, u32[]{:S(2)}, u32[]{:S(2)}) collective-permute-start(bf16[2,128,768]{2,1,0:T(8,128)(2,1)S(1)} %get-tuple-element.16), channel_id=1, source_target_pairs={{0,8},{8,0},{1,9},{9,1},{2,10},{10,2},{3,11},{11,3},{4,12},{12,4},... | collective-permute-start | bytes 1179656 | tf_op jit(solution)/shard_map/ppermute | solution.py:300
  104.6 32.8 %collective-permute-start.9 = (bf16[4,96,1024]{2,1,0:T(8,128)(2,1)}, bf16[4,96,1024]{2,1,0:T(8,128)(2,1)S(1)}, u32[]{:S(2)}, u32[]{:S(2)}) collective-permute-start(bf16[4,96,1024]{2,1,0:T(8,128)(2,1)} %get-tuple-element.19.refs_4_), channel_id=1, source_target_pairs={{0,2},{2,4},{4,6},{6,0},{1,3},{3,5},{5,7},{7,1},{8,10},{10,12},{12... | collective-permute-start | bytes 2359304 | tf_op jit(solution)/shard_map/ppermute | solution.py:283
  106.1 33.0 %collective-permute-start.10 = (bf16[4,96,1024]{2,1,0:T(8,128)(2,1)}, bf16[4,96,1024]{2,1,0:T(8,128)(2,1)S(1)}, u32[]{:S(2)}, u32[]{:S(2)}) collective-permute-start(bf16[4,96,1024]{2,1,0:T(8,128)(2,1)} %get-tuple-element.19.refs_4_), channel_id=1, source_target_pairs={{0,6},{2,0},{4,2},{6,4},{1,7},{3,1},{5,3},{7,5},{8,14},{10,8},{12,... | collective-permute-start | bytes 2359304 | tf_op jit(solution)/shard_map/ppermute | solution.py:284
  130.0 22.0 %collective-permute-start.14 = (bf16[4,96,1024]{2,1,0:T(8,128)(2,1)}, bf16[4,96,1024]{2,1,0:T(8,128)(2,1)}, u32[]{:S(2)}, u32[]{:S(2)}) collective-permute-start(bf16[4,96,1024]{2,1,0:T(8,128)(2,1)} %collective-permute-done.13.refs_9_), channel_id=1, source_target_pairs={{0,2},{2,4},{4,6},{6,0},{1,3},{3,5},{5,7},{7,1},{8,10},{10,12},{12... | collective-permute-start | bytes 2359304 | tf_op jit(solution)/shard_map/ppermute | solution.py:283
  131.5 22.6 %collective-permute-start.15 = (bf16[4,96,1024]{2,1,0:T(8,128)(2,1)}, bf16[4,96,1024]{2,1,0:T(8,128)(2,1)}, u32[]{:S(2)}, u32[]{:S(2)}) collective-permute-start(bf16[4,96,1024]{2,1,0:T(8,128)(2,1)} %collective-permute-done.13.refs_9_), channel_id=1, source_target_pairs={{0,6},{2,0},{4,2},{6,4},{1,7},{3,1},{5,3},{7,5},{8,14},{10,8},{12,... | collective-permute-start | bytes 2359304 | tf_op jit(solution)/shard_map/ppermute | solution.py:284
  134.0 24.8 %collective-permute-start.7 = (bf16[128,768]{1,0:T(8,128)(2,1)}, bf16[128,768]{1,0:T(8,128)(2,1)}, u32[]{:S(2)}, u32[]{:S(2)}) collective-permute-start(bf16[128,768]{1,0:T(8,128)(2,1)} %slice_bitcast_fusion), channel_id=1, source_target_pairs={{0,128},{128,0},{1,129},{129,1},{2,130},{130,2},{3,131},{131,3},{4... | collective-permute-start | bytes 589832 | tf_op jit(solution)/shard_map/ppermute | solution.py:301
  137.4 18.4 %copy-start.9 = (bf16[4,96,1024]{2,1,0:T(8,128)(2,1)}, bf16[4,96,1024]{2,1,0:T(8,128)(2,1)S(1)}, u32[]{:S(2)}) copy-start(bf16[4,96,1024]{2,1,0:T(8,128)(2,1)S(1)} %collective-permute-done.9.refs_5_) | copy-start | bytes 2359300
  138.2 30.2 %collective-permute-start.11 = (bf16[2,96,1024]{2,1,0:T(8,128)(2,1)}, bf16[2,96,1024]{2,1,0:T(8,128)(2,1)S(1)}, u32[]{:S(2)}, u32[]{:S(2)}) collective-permute-start(bf16[2,96,1024]{2,1,0:T(8,128)(2,1)} %slice.66), channel_id=1, source_target_pairs={{0,2},{2,4},{4,6},{6,0},{1,3},{3,5},{5,7},{7,1},{8,10},{10,12},{12... | collective-permute-start | bytes 1179656 | tf_op jit(solution)/shard_map/ppermute | solution.py:285
  139.1 20.7 %copy-start.10 = (bf16[4,96,1024]{2,1,0:T(8,128)(2,1)}, bf16[4,96,1024]{2,1,0:T(8,128)(2,1)S(1)}, u32[]{:S(2)}) copy-start(bf16[4,96,1024]{2,1,0:T(8,128)(2,1)S(1)} %collective-permute-done.10.refs_6_) | copy-start | bytes 2359300
  139.9 28.5 %collective-permute-start.12 = (bf16[2,96,1024]{2,1,0:T(8,128)(2,1)}, bf16[2,96,1024]{2,1,0:T(8,128)(2,1)S(1)}, u32[]{:S(2)}, u32[]{:S(2)}) collective-permute-start(bf16[2,96,1024]{2,1,0:T(8,128)(2,1)} %slice.67), channel_id=1, source_target_pairs={{0,6},{2,0},{4,2},{6,4},{1,7},{3,1},{5,3},{7,5},{8,14},{10,8},{12,... | collective-permute-start | bytes 1179656 | tf_op jit(solution)/shard_map/ppermute | solution.py:286
  153.8 14.6 %collective-permute-start.16 = (bf16[2,96,1024]{2,1,0:T(8,128)(2,1)}, bf16[2,96,1024]{2,1,0:T(8,128)(2,1)S(1)}, u32[]{:S(2)}, u32[]{:S(2)}) collective-permute-start(bf16[2,96,1024]{2,1,0:T(8,128)(2,1)} %slice.68), channel_id=1, source_target_pairs={{0,2},{2,4},{4,6},{6,0},{1,3},{3,5},{5,7},{7,1},{8,10},{10,12},{12... | collective-permute-start | bytes 1179656 | tf_op jit(solution)/shard_map/ppermute | solution.py:285
  155.8 12.6 %collective-permute-start.17 = (bf16[2,96,1024]{2,1,0:T(8,128)(2,1)}, bf16[2,96,1024]{2,1,0:T(8,128)(2,1)S(1)}, u32[]{:S(2)}, u32[]{:S(2)}) collective-permute-start(bf16[2,96,1024]{2,1,0:T(8,128)(2,1)} %slice.69), channel_id=1, source_target_pairs={{0,6},{2,0},{4,2},{6,4},{1,7},{3,1},{5,3},{7,5},{8,14},{10,8},{12,... | collective-permute-start | bytes 1179656 | tf_op jit(solution)/shard_map/ppermute | solution.py:286
  161.2 5.9 %collective-permute-start.8 = (bf16[128,256]{1,0:T(8,128)(2,1)S(1)}, bf16[128,256]{1,0:T(8,128)(2,1)S(1)}, u32[]{:S(2)}, u32[]{:S(2)}) collective-permute-start(bf16[128,256]{1,0:T(8,128)(2,1)S(1)} %slice_bitcast_fusion.2), channel_id=1, source_target_pairs={{0,128},{128,0},{1,129},{129,1},{2,130},{130,2},{3,131},{131,3},{4... | collective-permute-start | bytes 196616 | tf_op jit(solution)/shard_map/ppermute | solution.py:303
  168.4 0.7 copy-start.11
  168.4 0.9 copy-start.12
  168.4 1.0 copy-start.13
  168.4 1.1 copy-start.14
Sparse Core Ops, SparseCore 0:
  31.1 43.7 all-gather.4
  76.7 79.2 all-gather.6

commit v2 on v1

v2 whole, which is shorter than its diff:
```python
import functools

import jax
import jax.numpy as jnp
from jax import lax
from jax.experimental import pallas as pl
from jax.experimental.pallas import tpu as pltpu
from jax.sharding import Mesh, PartitionSpec as P

HEAD_DIM = 128
MEMBERS = 6
EXPERTS = 8
CAPACITY = 48
TOKENS = 128
SCALE = HEAD_DIM ** (-0.5)
LOG2E = 1.4426950408889634
SWAP = [(0, 1), (1, 0)]
RIGHT = [(i, (i + 1) % 4) for i in range(4)]
LEFT = [(i, (i - 1) % 4) for i in range(4)]
ACROSS = [(i, (i + 2) % 4) for i in range(4)]
Z = ("zq", "zl")
HALF = MEMBERS * HEAD_DIM
F32 = jnp.float32
BF16 = jnp.bfloat16


def vmem_specs(count):
    return [pl.BlockSpec(memory_space=pltpu.VMEM)] * count


def mxu(a, b, contract=((1,), (0,))):
    return lax.dot_general(a, b, (contract, ((), ())), preferred_element_type=F32)


def route_kernel(ids_ref, codes_ref, grad_ref, _, out_ref):
    expert = lax.broadcasted_iota(jnp.int32, (EXPERTS, TOKENS), 0)
    first = expert == ids_ref[0:1, :]
    second = expert == ids_ref[1:2, :]
    real = codes_ref[...].astype(F32) * (1.0 / 32768.0)
    hits = jnp.where(first, 1.0, 0.0) + jnp.where(second, 1.0, 0.0)
    scale = jnp.where(first, real[0:1, :], 0.0) + jnp.where(second, real[1:2, :], 0.0)
    earlier = lax.broadcasted_iota(jnp.int32, (TOKENS, TOKENS), 0)
    later = lax.broadcasted_iota(jnp.int32, (TOKENS, TOKENS), 1)
    before = jnp.where(earlier < later, 1.0, 0.0).astype(BF16)
    rank = mxu(hits.astype(BF16), before)
    rank = jnp.where(hits > 0.0, rank, -1.0)
    slot = lax.broadcasted_iota(jnp.int32, (CAPACITY, TOKENS), 0).astype(F32)
    grads = grad_ref[...]
    for e in range(EXPERTS):
        placed = rank[e : e + 1, :] == slot
        picked = mxu(jnp.where(placed, 1.0, 0.0).astype(BF16), grads)
        weight = jnp.sum(jnp.where(placed, scale[e : e + 1, :], 0.0), axis=1, keepdims=True)
        out_ref[e] = (picked * weight).astype(BF16)


def route(ids, codes, grads, after):
    return pl.pallas_call(
        route_kernel,
        out_shape=jax.ShapeDtypeStruct((EXPERTS, CAPACITY, grads.shape[1]), BF16),
        in_specs=vmem_specs(4),
        out_specs=vmem_specs(1)[0],
        compiler_params=pltpu.CompilerParams(vmem_limit_bytes=32 << 20),
        name="route",
    )(ids, codes, grads, after)


def pair_kernel(place_ref, key_ref, value_ref, keep_ref, send_ref):
    xh = place_ref[0]
    for side, out_ref in ((xh, keep_ref), (1 - xh, send_ref)):
        columns = pl.ds(pl.multiple_of(side * HEAD_DIM, HEAD_DIM), HEAD_DIM)
        out_ref[:, 0:HEAD_DIM] = key_ref[:, columns]
        out_ref[:, HEAD_DIM:] = value_ref[:, columns]


def pair(xh, key, value):
    shape = jax.ShapeDtypeStruct(key.shape, BF16)
    return pl.pallas_call(
        pair_kernel,
        out_shape=(shape, shape),
        in_specs=[pl.BlockSpec(memory_space=pltpu.SMEM)] + vmem_specs(2),
        out_specs=tuple(vmem_specs(2)),
        name="pair",
    )(xh[None], key, value)


def halves_kernel(place_ref, hidden_ref, _, keep_ref, send_ref):
    dp = place_ref[0]
    for side, out_ref in ((dp, keep_ref), (1 - dp, send_ref)):
        columns = pl.ds(pl.multiple_of(side * 1024, 1024), 1024)
        for part in range(2):
            rows = slice(part * CAPACITY, (part + 1) * CAPACITY)
            out_ref[0, rows, :] = hidden_ref[part, 0, :, columns]


def halves(dp, hidden, after):
    shape = jax.ShapeDtypeStruct((4, 2 * CAPACITY, 1024), BF16)
    block = pl.BlockSpec((1, 2 * CAPACITY, 1024), lambda m: (m, 0, 0))
    return pl.pallas_call(
        halves_kernel,
        grid=(4,),
        out_shape=(shape, shape),
        in_specs=[
            pl.BlockSpec(memory_space=pltpu.SMEM),
            pl.BlockSpec((2, 1, CAPACITY, 2048), lambda m: (0, m, 0, 0)),
            pl.BlockSpec(memory_space=pl.ANY),
        ],
        out_specs=(block, block),
        name="halves",
    )(dp[None], hidden, after)


def pack_kernel(
    place_ref, query_ref, grad_ref, out_ref, norms_ref, _, keep_ref, send_ref, token_ref, delta_ref
):
    token_ref[...] = jnp.zeros_like(token_ref)
    xh = place_ref[0]
    for head in range(2 * MEMBERS):
        columns = slice(head * HEAD_DIM, (head + 1) * HEAD_DIM)
        product = grad_ref[:, columns].astype(F32) * out_ref[:, columns].astype(F32)
        delta_ref[head // MEMBERS, head % MEMBERS : head % MEMBERS + 1, :] = jnp.sum(
            product.T, axis=0, keepdims=True
        )
    for side, pack_ref in ((xh, keep_ref), (1 - xh, send_ref)):
        columns = pl.ds(pl.multiple_of(side * HALF, HEAD_DIM), HALF)
        pack_ref[0:TOKENS, 0:HALF] = query_ref[:, columns]
        pack_ref[0:TOKENS, HALF : 2 * HALF] = grad_ref[:, columns]
        rest = jnp.concatenate([norms_ref[side] * LOG2E, delta_ref[side]], axis=0)
        pack_ref[TOKENS : TOKENS + 16, :] = jnp.zeros((16, 2 * HALF), BF16)
        for term in range(3):
            part = rest.astype(BF16)
            pack_ref[TOKENS : TOKENS + 16, term * TOKENS : (term + 1) * TOKENS] = part
            rest = rest - part.astype(F32)


def pack(xh, query, grad, out, norms, after):
    shape = jax.ShapeDtypeStruct((TOKENS + 16, query.shape[1]), BF16)
    return pl.pallas_call(
        pack_kernel,
        out_shape=(shape, shape, jax.ShapeDtypeStruct((8, HEAD_DIM), F32)),
        in_specs=[pl.BlockSpec(memory_space=pltpu.SMEM)]
        + vmem_specs(4)
        + [pl.BlockSpec(memory_space=pl.ANY)],
        out_specs=tuple(vmem_specs(3)),
        scratch_shapes=[pltpu.VMEM((2, 8, TOKENS), F32)],
        compiler_params=pltpu.CompilerParams(vmem_limit_bytes=32 << 20),
        name="pack",
    )(xh[None], query, grad, out, norms, after)


def attention_kernel(
    place_ref, kv_ref, p00, p01, p10, p11, *refs
):
    dkv_ref, keep_ref, send_ref = refs[-11:-8]
    q_ref, do_ref, qt_ref, dot_ref, dqt_ref, rows_ref, diff_ref, acc_ref = refs[-8:]
    xh, z, co = place_ref[0], place_ref[1], place_ref[2]
    packs = ((p00, p01), (p10, p11))
    for g in range(2):
        for c in range(2):
            span = slice(c * TOKENS, (c + 1) * TOKENS)
            terms = packs[g][c][TOKENS : TOKENS + 16, 0 : 3 * TOKENS].astype(F32)
            rows_ref[g, :, span] = (
                terms[:, 0:TOKENS] + terms[:, TOKENS : 2 * TOKENS] + terms[:, 2 * TOKENS :]
            )
            for h in range(MEMBERS):
                block = packs[g][c][:TOKENS, h * HEAD_DIM : (h + 1) * HEAD_DIM]
                q_ref[g, h, span, :] = block
                qt_ref[g, h, :, span] = block.T
                block = packs[g][c][:TOKENS, HALF + h * HEAD_DIM : HALF + (h + 1) * HEAD_DIM]
                do_ref[g, h, span, :] = block
                dot_ref[g, h, :, span] = block.T
    dqt_ref[...] = jnp.zeros_like(dqt_ref)
    key_row = lax.broadcasted_iota(jnp.int32, (256, 256), 0)
    query_row = lax.broadcasted_iota(jnp.int32, (256, 256), 1)
    own = query_row < TOKENS
    query_at = jnp.where(own, query_row + co * TOKENS, query_row - TOKENS + (1 - co) * TOKENS)
    diff_ref[...] = query_at - jnp.where(key_row < TOKENS, key_row, key_row + TOKENS)

    def chunk(index, _):
        slot, t = index // 4, index % 4
        xh_key = jnp.where(slot == 0, xh, 1 - xh)
        kv = kv_ref[pl.ds(2 * t, 2), slot].reshape(256, 256)
        key, value = kv[:, :HEAD_DIM], kv[:, HEAD_DIM:]
        key_t = key.T
        acc_ref[...] = jnp.zeros_like(acc_ref)
        for g in range(2):
            xh_query = xh if g == 0 else 1 - xh
            seen = (xh_key < xh_query) | ((xh_key == xh_query) & (t <= z // 2))
            bound = (xh_key - xh_query) * 2048 + t * 512 + co * TOKENS - z * 256

            @pl.when(seen)
            def _():
                key_part = jnp.zeros((256, HEAD_DIM), F32)
                value_part = jnp.zeros((256, HEAD_DIM), F32)
                for h in range(MEMBERS):
                    scores = mxu(key, qt_ref[g, h])
                    exp_scores = jnp.exp2(scores * (SCALE * LOG2E) - rows_ref[g, h : h + 1, :])
                    exp_scores = jnp.where(diff_ref[...] >= bound, exp_scores, 0.0)
                    prob_grad = mxu(value, dot_ref[g, h])
                    value_part += mxu(exp_scores.astype(BF16), do_ref[g, h])
                    score_grad = (
                        (SCALE * exp_scores) * (prob_grad - rows_ref[g, 8 + h : 9 + h, :])
                    ).astype(BF16)
                    key_part += mxu(score_grad, q_ref[g, h])
                    dqt_ref[g, h] += mxu(key_t, score_grad)
                acc_ref[:, :HEAD_DIM] += key_part
                acc_ref[:, HEAD_DIM:] += value_part

        dkv_ref[pl.ds(2 * t, 2), slot] = acc_ref[...].astype(BF16).reshape(2, TOKENS, 256)
        return 0

    lax.fori_loop(0, 8, chunk, 0)
    for g in range(2):
        for h in range(MEMBERS):
            columns = slice(h * HEAD_DIM, (h + 1) * HEAD_DIM)
            total = dqt_ref[g, h]
            keep_ref[g, :, columns] = total[:, :TOKENS].T
            send_ref[g, :, columns] = total[:, TOKENS:].T.astype(BF16)


def attention(place, kv, packs, after):
    return pl.pallas_call(
        attention_kernel,
        out_shape=(
            jax.ShapeDtypeStruct((8, 2, TOKENS, 256), BF16),
            jax.ShapeDtypeStruct((2, TOKENS, HALF), F32),
            jax.ShapeDtypeStruct((2, TOKENS, HALF), BF16),
        ),
        in_specs=[pl.BlockSpec(memory_space=pltpu.SMEM)]
        + vmem_specs(5)
        + [pl.BlockSpec(memory_space=pl.ANY)] * len(after),
        out_specs=tuple(vmem_specs(3)),
        scratch_shapes=[
            pltpu.VMEM((2, MEMBERS, 256, HEAD_DIM), BF16),
            pltpu.VMEM((2, MEMBERS, 256, HEAD_DIM), BF16),
            pltpu.VMEM((2, MEMBERS, HEAD_DIM, 256), BF16),
            pltpu.VMEM((2, MEMBERS, HEAD_DIM, 256), BF16),
            pltpu.VMEM((2, MEMBERS, HEAD_DIM, 256), F32),
            pltpu.VMEM((2, 16, 256), F32),
            pltpu.VMEM((256, 256), jnp.int32),
            pltpu.VMEM((256, 256), F32),
        ],
        cost_estimate=pl.CostEstimate(
            flops=16_000_000_000, transcendentals=5_000_000, bytes_accessed=8_000_000
        ),
        compiler_params=pltpu.CompilerParams(vmem_limit_bytes=48 << 20),
        name="attention",
    )(place, kv, *packs, *after)


ANY = pl.BlockSpec(memory_space=pl.ANY)
HALF_COST = 6
KV_COST = 10


def joined_kernel(keep_ref, other_ref, out_ref):
    out_ref[0] = keep_ref[...]
    out_ref[1] = other_ref[...]


def joined(keep, other):
    return pl.pallas_call(
        joined_kernel,
        out_shape=jax.ShapeDtypeStruct((2,) + keep.shape, keep.dtype),
        in_specs=vmem_specs(2),
        out_specs=vmem_specs(1)[0],
        name="joined",
    )(keep, other)


def mark_kernel(_, out_ref):
    out_ref[...] = jnp.zeros_like(out_ref)


def mark(after, cost):
    return pl.pallas_call(
        mark_kernel,
        out_shape=jax.ShapeDtypeStruct((8, HEAD_DIM), F32),
        in_specs=[ANY],
        out_specs=vmem_specs(1)[0],
        cost_estimate=pl.CostEstimate(
            flops=cost * 1_000_000_000, transcendentals=0, bytes_accessed=1_000_000
        ),
        name="mark",
    )(after)


def half_kernel(first, rows_ref, out_ref):
    out_ref[...] = rows_ref[first : first + 2]


def half(rows, first, cost=HALF_COST):
    shape = (2,) + rows.shape[1:]
    return pl.pallas_call(
        functools.partial(half_kernel, first),
        out_shape=jax.ShapeDtypeStruct(shape, rows.dtype),
        in_specs=vmem_specs(1),
        out_specs=vmem_specs(1)[0],
        cost_estimate=pl.CostEstimate(
            flops=cost * 1_000_000_000, transcendentals=0, bytes_accessed=2_000_000
        ),
        name="half",
    )(rows)


def down_kernel(shards, place_ref, *refs):
    hidden, (out_ref, gathered_ref) = (refs[-10:-6], refs[-6:-2]), refs[-2:]
    routed = refs[:-10]
    tp, zl, co = (place_ref[i] for i in range(3))

    @pl.when(pl.program_id(0) == 0)
    def _():
        for n, (other_seq, other_z, other_core) in enumerate(shards):
            m = 2 * (1 - zl if other_z else zl) + (1 - co if other_core else co)
            for piece, step in zip(hidden[other_seq], (0, 3, 1, 2)):
                gathered_ref[n, lax.rem(tp + step, 4)] = piece[m]

    left_side = gathered_ref[...].reshape(len(shards) * 384, gathered_ref.shape[3])
    right_side = jnp.concatenate([r[...].reshape(-1, out_ref.shape[1]) for r in routed], axis=0)
    out_ref[...] = mxu(left_side, right_side, ((0,), (0,))).astype(BF16)


def down(place, shards, routed, hidden, tile=512):
    width = routed[0].shape[-1]
    rows = hidden[0].shape[-1]
    whole = pl.BlockSpec((4, 96, rows), lambda i, p: (0, 0, 0), pipeline_mode=pl.Buffered(1))
    return pl.pallas_call(
        functools.partial(down_kernel, shards),
        grid_spec=pltpu.PrefetchScalarGridSpec(
            num_scalar_prefetch=1,
            grid=(width // tile,),
            in_specs=[pl.BlockSpec(r.shape[:2] + (tile,), lambda i, p: (0, 0, i)) for r in routed]
            + [whole] * 8,
            out_specs=pl.BlockSpec((rows, tile), lambda i, p: (0, i)),
            scratch_shapes=[pltpu.VMEM((len(shards), 4, 96, rows), BF16)],
        ),
        out_shape=jax.ShapeDtypeStruct((rows, width), BF16),
        cost_estimate=pl.CostEstimate(
            flops=16_000_000_000, transcendentals=0, bytes_accessed=20_000_000
        ),
        compiler_params=pltpu.CompilerParams(vmem_limit_bytes=56 << 20),
        name="down",
    )(place, *routed, *hidden)


def finish_kernel(parts_ref, kept_ref, near_ref, mine_ref, send_ref):
    for side, out_ref in ((0, mine_ref), (1, send_ref)):
        out_ref[:, 0:HALF] = (kept_ref[side] + near_ref[side].astype(F32)).astype(BF16)
        total = parts_ref[0, side].astype(F32)
        for part in range(1, 8):
            total = total + parts_ref[part, side].astype(F32)
        out_ref[:, HALF:] = total.astype(BF16)


def finish(parts, kept, near):
    shape = jax.ShapeDtypeStruct((TOKENS, HALF + 256), BF16)
    return pl.pallas_call(
        finish_kernel,
        out_shape=(shape, shape),
        in_specs=vmem_specs(3),
        out_specs=tuple(vmem_specs(2)),
        compiler_params=pltpu.CompilerParams(vmem_limit_bytes=32 << 20),
        name="finish",
    )(parts, kept, near)


def spread_kernel(place_ref, mine_ref, other_ref, _, query_ref, key_ref, value_ref):
    xh = place_ref[0]
    for side, from_ref in ((xh, mine_ref), (1 - xh, other_ref)):
        wide = pl.ds(pl.multiple_of(side * HALF, HEAD_DIM), HALF)
        narrow = pl.ds(pl.multiple_of(side * HEAD_DIM, HEAD_DIM), HEAD_DIM)
        query_ref[:, wide] = from_ref[:, 0:HALF]
        key_ref[:, narrow] = from_ref[:, HALF : HALF + HEAD_DIM]
        value_ref[:, narrow] = from_ref[:, HALF + HEAD_DIM :]


def spread(xh, mine, other, after):
    shape = lambda width: jax.ShapeDtypeStruct((TOKENS, width), BF16)
    return pl.pallas_call(
        spread_kernel,
        out_shape=(shape(2 * HALF), shape(256), shape(256)),
        in_specs=[pl.BlockSpec(memory_space=pltpu.SMEM)] + vmem_specs(2) + [ANY],
        out_specs=tuple(vmem_specs(3)),
        name="spread",
    )(xh[None], mine, other, after)


def local(
    query_rows,
    key_rows,
    value_rows,
    attention_out,
    output_grad,
    log_norms,
    moe_grad,
    expert_ids,
    route_weight,
    hidden_act,
):
    xh, zl, co, dp, tp = (lax.axis_index(name) for name in ("xh", "zl", "co", "dp", "tp"))
    z = lax.axis_index(Z)

    kv_keep, kv_send = pair(xh, key_rows[0], value_rows[0])
    kv = joined(kv_keep, lax.ppermute(kv_send, "xh", SWAP))
    kv_all = lax.all_gather(kv, Z, axis=0)

    corner = lambda arrays: sum(rows[0, :16, :HEAD_DIM] for rows in arrays)

    norms = jnp.pad(log_norms[0].T.reshape(2, MEMBERS, TOKENS), ((0, 0), (0, 2), (0, 0)))
    keep, send, packed = pack(
        xh, query_rows[0], output_grad[0], attention_out[0], norms, kv_keep
    )
    across = lax.ppermute(send, "xh", SWAP)

    outgoing = route(expert_ids[0].T, route_weight[0].T, moe_grad[0], packed)
    routed = lax.all_to_all(outgoing, ("xh", "zq"), 0, 0, tiled=True)
    routed = routed.reshape(4, 2 * CAPACITY, moe_grad.shape[2])
    by_x = lax.ppermute(routed, "dp", SWAP)
    by_z = lax.ppermute(routed, "zl", SWAP)
    diagonal = (lax.ppermute(half(by_z, 0), "dp", SWAP), lax.ppermute(half(by_x, 2), "zl", SWAP))
    shards = (routed, by_x, by_z) + diagonal
    shards += tuple(lax.ppermute(rows, "co", SWAP) for rows in shards)

    hidden = hidden_act[0].reshape(2, 4, CAPACITY, 2048)
    hidden, hidden_send = halves(dp, hidden, corner([across[None]]) + corner([outgoing]))
    hidden_other = lax.ppermute(hidden_send, "dp", SWAP)
    own = [hidden] + [lax.ppermute(hidden, "tp", move) for move in (RIGHT, LEFT, ACROSS)]
    other = [hidden_other] + [
        lax.ppermute(hidden_other, "tp", move) for move in (RIGHT, LEFT, ACROSS)
    ]

    packs = (keep, lax.ppermute(keep, "co", SWAP), across, lax.ppermute(across, "co", SWAP))
    early = corner([hidden_other] + own[1:])
    dkv, dq_keep, dq_send = attention(
        jnp.stack([xh, z, co]), kv_all, packs, [early, mark(kv_all, KV_COST)]
    )
    dq_near = lax.ppermute(dq_send, "co", SWAP)
    dkv = lax.all_to_all(dkv, Z, 0, 0, tiled=True)
    mine, send = finish(dkv, dq_keep, dq_near)

    names = tuple((seq, z, core) for core in (0, 1) for seq, z in ((0, 0), (1, 0), (0, 1), (1, 1)))
    down_grad = down(jnp.stack([tp, zl, co]), names, shards, own + other)
    grads = spread(xh, mine, lax.ppermute(send, "xh", SWAP), down_grad)
    return tuple(grad[None] for grad in grads) + (down_grad,)


def solution(mesh):
    fine = Mesh(mesh.devices.reshape(2, 4, 2, 2, 4, 2), ("xh", "zq", "zl", "co", "tp", "dp"))
    cp = ("xh", "zq", "zl", "co")
    return jax.shard_map(
        local,
        mesh=fine,
        in_specs=(
            P("dp", cp, "tp"),
            P("dp", cp, "tp"),
            P("dp", cp, "tp"),
            P("dp", cp, "tp"),
            P("dp", cp, "tp"),
            P("dp", cp, "tp"),
            P("dp", cp, "tp"),
            P("dp", cp, None),
            P("dp", cp, None),
            P("dp", "tp", cp),
        ),
        out_specs=(
            P("dp", cp, "tp"),
            P("dp", cp, "tp"),
            P("dp", cp, "tp"),
            P(cp + ("dp",), "tp"),
        ),
        check_vma=False,
    )
```

time: 193 us -> 187 us (0.969); the launches traced: 193 us -> 183 us
  Pallas kernels: 31 us -> 44.9 us
  waiting for transfers between devices: 72.8 us -> 60.4 us
  local copies, waits for them, and re-layouts: 17.6 us -> 12.6 us
  other arithmetic: 5.83 us -> 2.67 us
  starting transfers between devices: 51.2 us -> 48.6 us
    all_to_all x2, waiting for transfers between devices: 24.7 us -> 0.01 us  [the longest x1 0.01 us: local(): dkv = lax.all_to_all(dkv, Z, 0, 0, tiled=True)]
    ppermute x15 -> x19, waiting for transfers between devices: 39 us -> 60.4 us  [the longest x3 25.7 us: local(): lax.ppermute(hidden, 'tp', move)]
    pallas_call x3 -> x11, Pallas kernels: 29.3 us -> 43.2 us  [the longest x1 16.7 us: down(): pl.pallas_call(functools.partial(down_kernel, shards), grid_spec=pltpu.Pr...]
    ppermute x1, waiting for transfers between devices: 7.35 us -> 0.01 us  [local(): across = lax.ppermute(send, 'xh', SWAP)]
    ppermute x15 -> x19, starting transfers between devices: 26.7 us -> 19.5 us  [the longest x3 5.22 us: local(): lax.ppermute(hidden, 'tp', move)]
    unnamed x39 -> x41, local copies, waits for them, and re-layouts: 5.93 us -> 12.6 us
    slice x5 -> x0, local copies, waits for them, and re-layouts: 5.2 us -> none  [the longest x2 2.59 us: local(): far_high = lax.ppermute(right[2:], 'tp', LEFT)]
    another operation x3 -> x0, local copies, waits for them, and re-layouts: 3.08 us -> none  [the longest x1 2.87 us: local(): hidden_act[0].reshape(2, 4, CAPACITY, 2, 1024).transpose(3, 1, 0, 2, 4)]
  transfers between devices with their start and end apart: 22 -> 25, of which waited for: 8 -> 6; matrix products, arithmetic and copies ran while one was open for 9% -> 2% of each run, Pallas kernels for 7% -> 22%
where the time goes in v2:
time: 187 us; the launch traced here: 183 us
  waiting for transfers between devices  60.4 us (32%)
  starting transfers between devices  48.6 us (26%)
  Pallas kernels  44.9 us (24%)
  between operations  14.2 us (8%)
  local copies, waits for them, and re-layouts  12.6 us (7%)
  other arithmetic  2.67 us (1%)
    ppermute x3, waiting for transfers between devices, local(): lax.ppermute(hidden, 'tp', move)  25.7 us
    all_to_all x1, starting transfers between devices, local(): dkv = lax.all_to_all(dkv, Z, 0, 0, tiled=True)  18.4 us
    pallas_call x1, Pallas kernels, down(): pl.pallas_call(functools.partial(down_kernel, shards), grid_spec=pltpu.Pr...  16.7 us
    ppermute x1, waiting for transfers between devices, local(): lax.ppermute(half(by_z, 0), 'dp', SWAP)  14.6 us
    ppermute x1, waiting for transfers between devices, local(): lax.ppermute(half(by_x, 2), 'zl', SWAP)  13.2 us
    unnamed x41, local copies, waits for them, and re-layouts  12.6 us
    pallas_call x1, Pallas kernels, attention(): pl.pallas_call(attention_kernel, out_shape=(jax.ShapeDtypeStruct((8, 2, T...  12.5 us
    all_to_all x1, starting transfers between devices, local(): routed = lax.all_to_all(outgoing, ('xh', 'zq'), 0, 0, tiled=True)  7.57 us
  transfers between devices with their start and end apart: 25, of which 6 were waited for; matrix products, arithmetic and copies ran while one was open for 2% of the time, Pallas kernels for 22%

profile of v2, /device:TPU:32, one launch (start us, length us, event | category | flops | bytes accessed | tf_op | source)
XLA Modules:
  0.0 183.3 jit_solution(1054530892801557838)
XLA Ops:
  7.2 0.0 all-gather.3.cloned.1.call-start
  7.2 1.6 pair.1
  8.8 3.0 %collective-permute-start = (bf16[128,256]{1,0:T(8,128)(2,1)}, bf16[128,256]{1,0:T(8,128)(2,1)S(1)}, u32[]{:S(2)}, u32[]{:S(2)}) collective-permute-start(bf16[128,256]{1,0:T(8,128)(2,1)} %get-tuple-element.20), channel_id=1, source_target_pairs={{0,128},{128,0},{1,129},{129,1},{2,130},{130,2},{3,131},{131,3},{4... | collective-permute-start | bytes 196616 | tf_op jit(solution)/shard_map/ppermute | solution.py:403
  11.9 3.0 %collective-permute-done.other_ref = bf16[128,256]{1,0:T(8,128)(2,1)S(1)} collective-permute-done((bf16[128,256]{1,0:T(8,128)(2,1)}, bf16[128,256]{1,0:T(8,128)(2,1)S(1)}, u32[]{:S(2)}, u32[]{:S(2)}) %collective-permute-start) | collective-permute-done | bytes 65568 | tf_op jit(solution)/shard_map/ppermute | solution.py:403
  14.8 0.6 copy-done.17
  15.5 1.5 joined.1
  17.0 0.0 all-gather.3.cloned.1.call-update
  17.0 0.7 copy.16
  17.7 1.0 copy-done
  18.7 1.0 copy-done.1
  19.7 1.0 copy-done.2
  20.7 0.8 copy-done.4
  21.6 0.3 pack.1
  21.8 3.1 %collective-permute-start.2 = (bf16[144,1536]{1,0:T(8,128)(2,1)S(1)}, bf16[144,1536]{1,0:T(8,128)(2,1)S(1)}, u32[]{:S(2)}, u32[]{:S(2)}) collective-permute-start(bf16[144,1536]{1,0:T(8,128)(2,1)S(1)} %get-tuple-element.22), channel_id=1, source_target_pairs={{0,128},{128,0},{1,129},{129,1},{2,130},{130,2},{3,131},{131,3},{4... | collective-permute-start | bytes 1327112 | tf_op jit(solution)/shard_map/ppermute | solution.py:412
  25.0 1.7 route.1
  26.7 7.6 %all-to-all-start.1 = ((bf16[8,48,1536]{2,1,0:T(8,128)(2,1)}), bf16[8,48,1536]{2,1,0:T(8,128)(2,1)}, u32[]{:S(2)}, u32[]{:S(2)}) async-start(bf16[8,48,1536]{2,1,0:T(8,128)(2,1)} %route.1), calls=%async_computation.1 | async-start | bytes 2359296 | tf_op jit(solution)/shard_map/all_to_all | solution.py:415
  34.2 0.0 collective-permute-done.2.p10
  34.2 1.3 fusion.1._
  35.5 3.6 %halves.1 = (bf16[4,96,1024]{2,1,0:T(8,128)(2,1)}, bf16[4,96,1024]{2,1,0:T(8,128)(2,1)}) custom-call(s32[1]{0:T(128)} %bitcast.10.place_ref, bf16[2,4,48,2048]{3,2,1,0:T(8,128)(2,1)} %bitcast.43, bf16[16,128]{1,0:T(8,128)(2,1)} %fusion.1._), custom_call_target="tpu_custom_call" | custom-call | tf_op jit(solution)/shard_map/halves/pallas_call | solution.py:98
  39.1 3.2 %collective-permute-start.7 = (bf16[4,96,1024]{2,1,0:T(8,128)(2,1)}, bf16[4,96,1024]{2,1,0:T(8,128)(2,1)S(1)}, u32[]{:S(2)}, u32[]{:S(2)}) collective-permute-start(bf16[4,96,1024]{2,1,0:T(8,128)(2,1)} %get-tuple-element.25.refs_10_), channel_id=1, source_target_pairs={{0,4},{2,6},{4,0},{6,2},{1,5},{3,7},{5,1},{7,3},{8,12},{10,14},{12... | collective-permute-start | bytes 2359304 | tf_op jit(solution)/shard_map/ppermute | solution.py:426
  42.3 1.4 collective-permute-start.4
  43.8 1.1 collective-permute-start.6
  44.8 1.0 collective-permute-start.5
  45.8 0.0 collective-permute-start.1
  45.8 0.1 add_add_fusion.place_ref
  45.9 15.5 %collective-permute-done.7.refs_13_ = bf16[4,96,1024]{2,1,0:T(8,128)(2,1)S(1)} collective-permute-done((bf16[4,96,1024]{2,1,0:T(8,128)(2,1)}, bf16[4,96,1024]{2,1,0:T(8,128)(2,1)S(1)}, u32[]{:S(2)}, u32[]{:S(2)}) %collective-permute-start.7) | collective-permute-done | bytes 786464 | tf_op jit(solution)/shard_map/ppermute | solution.py:426
  61.4 4.0 %collective-permute-done.4.refs_14_ = bf16[4,96,1024]{2,1,0:T(8,128)(2,1)} collective-permute-done((bf16[4,96,1024]{2,1,0:T(8,128)(2,1)}, bf16[4,96,1024]{2,1,0:T(8,128)(2,1)}, u32[]{:S(2)}, u32[]{:S(2)}) %collective-permute-start.4) | collective-permute-done | bytes 786464 | tf_op jit(solution)/shard_map/ppermute | solution.py:425
  65.4 0.2 collective-permute-start.19
  65.6 10.2 %collective-permute-done.6.refs_12_ = bf16[4,96,1024]{2,1,0:T(8,128)(2,1)} collective-permute-done((bf16[4,96,1024]{2,1,0:T(8,128)(2,1)}, bf16[4,96,1024]{2,1,0:T(8,128)(2,1)}, u32[]{:S(2)}, u32[]{:S(2)}) %collective-permute-start.6) | collective-permute-done | bytes 786464 | tf_op jit(solution)/shard_map/ppermute | solution.py:426
  75.8 2.6 %collective-permute-start.20 = (bf16[4,96,1024]{2,1,0:T(8,128)(2,1)}, bf16[4,96,1024]{2,1,0:T(8,128)(2,1)}, u32[]{:S(2)}, u32[]{:S(2)}) collective-permute-start(bf16[4,96,1024]{2,1,0:T(8,128)(2,1)} %collective-permute-done.4.refs_14_), channel_id=1, source_target_pairs={{0,6},{2,0},{4,2},{6,4},{1,7},{3,1},{5,3},{7,5},{8,14},{10,8},{12,... | collective-permute-start | bytes 2359304 | tf_op jit(solution)/shard_map/ppermute | solution.py:428
  78.4 0.6 collective-permute-start.21
  79.0 0.7 fusion.refs_0_
  79.8 0.6 mark.1.refs_1_
  80.4 0.0 collective-permute-done.1.p01
  80.4 0.8 copy-done.9
  81.2 1.4 collective-permute-start.10
  82.6 0.0 collective-permute-done.3.p11
  82.6 0.8 copy-done.11
  83.4 1.0 collective-permute-start.11
  84.4 1.0 copy-done.10
  85.4 1.0 copy-done.12
  86.4 0.7 copy-done.15
  87.1 12.5 %attention.1 = (bf16[8,2,128,256]{3,2,1,0:T(8,128)(2,1)}, f32[2,128,768]{2,1,0:T(8,128)S(1)}, bf16[2,128,768]{2,1,0:T(8,128)(2,1)S(1)}) custom-call(s32[3]{0:T(128)S(1)} %add_add_fusion.place_ref, bf16[8,2,128,256]{3,2,1,0:T(8,128)(2,1)S(1)} %bitcast.42, bf16[144,1536]{1,0:T(8,128)(2,1)S(1)} %get-tuple-element.21.p00, bf16[144,1536]{1,0:T(8,128)(2,1)S(1)} %copy-done.10, ...), custom_call_target="tpu_custom_call" | custom-call | flops 16000000000 | bytes 8000000 | tf_op jit(solution)/shard_map/attention/pallas_call | solution.py:221
  99.7 0.7 copy-done.13
  100.4 18.4 %all-to-all-start = ((bf16[8,2,128,256]{3,2,1,0:T(8,128)(2,1)}), bf16[8,2,128,256]{3,2,1,0:T(8,128)(2,1)S(1)}, u32[]{:S(2)}, u32[]{:S(2)}) async-start(bf16[8,2,128,256]{3,2,1,0:T(8,128)(2,1)} %get-tuple-element.26), calls=%async_computation | async-start | bytes 2097152 | tf_op jit(solution)/shard_map/all_to_all | solution.py:437
  118.8 0.0 collective-permute-done.11.rows_ref.refs_2_
  118.8 0.1 collective-permute-start.8
  118.9 2.1 %half.2 = bf16[2,96,1536]{2,1,0:T(8,128)(2,1)} custom-call(bf16[4,96,1536]{2,1,0:T(8,128)(2,1)} %collective-permute-done.11.rows_ref.refs_2_), custom_call_target="tpu_custom_call" | custom-call | flops 6000000000 | bytes 2000000 | tf_op jit(solution)/shard_map/half/pallas_call | solution.py:293
  121.0 0.5 collective-permute-start.14
  121.5 2.1 %half.3 = bf16[2,96,1536]{2,1,0:T(8,128)(2,1)} custom-call(bf16[4,96,1536]{2,1,0:T(8,128)(2,1)} %collective-permute-done.10.rows_ref.refs_1_), custom_call_target="tpu_custom_call" | custom-call | flops 6000000000 | bytes 2000000 | tf_op jit(solution)/shard_map/half/pallas_call | solution.py:293
  123.6 0.4 collective-permute-start.12
  124.0 0.0 collective-permute-start.13
  124.1 0.1 collective-permute-start.15
  124.2 0.5 collective-permute-start.16
  124.7 14.6 %collective-permute-done.12.refs_3_ = bf16[2,96,1536]{2,1,0:T(8,128)(2,1)} collective-permute-done((bf16[2,96,1536]{2,1,0:T(8,128)(2,1)}, bf16[2,96,1536]{2,1,0:T(8,128)(2,1)}, u32[]{:S(2)}, u32[]{:S(2)}) %collective-permute-start.12) | collective-permute-done | bytes 589856 | tf_op jit(solution)/shard_map/ppermute | solution.py:419
  139.2 13.2 %collective-permute-done.13.refs_4_ = bf16[2,96,1536]{2,1,0:T(8,128)(2,1)} collective-permute-done((bf16[2,96,1536]{2,1,0:T(8,128)(2,1)}, bf16[2,96,1536]{2,1,0:T(8,128)(2,1)}, u32[]{:S(2)}, u32[]{:S(2)}) %collective-permute-start.13) | collective-permute-done | bytes 589856 | tf_op jit(solution)/shard_map/ppermute | solution.py:419
  152.4 0.6 add_add_fusion.1.place_ref
  153.0 0.2 finish.1
  153.2 0.7 copy-done.5
  153.9 2.3 %collective-permute-start.9 = (bf16[128,1024]{1,0:T(8,128)(2,1)S(1)}, bf16[128,1024]{1,0:T(8,128)(2,1)S(1)}, u32[]{:S(2)}, u32[]{:S(2)}) collective-permute-start(bf16[128,1024]{1,0:T(8,128)(2,1)S(1)} %get-tuple-element.30), channel_id=1, source_target_pairs={{0,128},{128,0},{1,129},{129,1},{2,130},{130,2},{3,131},{131,3},{4... | collective-permute-start | bytes 786440 | tf_op jit(solution)/shard_map/ppermute | solution.py:442
  156.2 1.0 copy-done.19
  157.2 16.7 %down.1._ = bf16[1024,1536]{1,0:T(8,128)(2,1)} custom-call(s32[3]{0:T(128)} %add_add_fusion.1.place_ref, bf16[4,96,1536]{2,1,0:T(8,128)(2,1)} %bitcast.22.refs_0_, bf16[4,96,1536]{2,1,0:T(8,128)(2,1)} %collective-permute-done.10.rows_ref.refs_1_, bf16[4,96,1536]{2,1,0:T(8,128)(2,1)} %collective-permute-done.11.rows_ref.refs_2_, ...), custom_call_target="tpu_custom_call" | custom-call | flops 16000000000 | bytes 20000000 | tf_op jit(solution)/shard_map/down/pallas_call | solution.py:326
  174.0 0.7 copy-done.16
  174.7 1.8 %spread.1 = (bf16[128,1536]{1,0:T(8,128)(2,1)}, bf16[128,256]{1,0:T(8,128)(2,1)}, bf16[128,256]{1,0:T(8,128)(2,1)}) custom-call(s32[1]{0:T(128)} %bitcast.place_ref, bf16[128,1024]{1,0:T(8,128)(2,1)} %copy-done.5, bf16[128,1024]{1,0:T(8,128)(2,1)} %copy-done.16, bf16[1024,1536]{1,0:T(8,128)(2,1)} %down.1._), custom_call_target="tpu_custom_call" | custom-call | tf_op jit(solution)/shard_map/spread/pallas_call | solution.py:378
  (46 shorter events, 0.1 us)
Async XLA Ops:
  7.2 17.8 %copy-start.6 = (s32[1,128,2]{1,2,0:T(2,128)S(1)}, s32[1,128,2]{1,2,0:T(2,128)}, u32[]{:S(2)}) copy-start(s32[1,128,2]{1,2,0:T(2,128)} %param.17) | copy-start | bytes 3076
  7.2 17.8 %copy-start.7 = (s32[1,128,2]{1,2,0:T(2,128)S(1)}, s32[1,128,2]{1,2,0:T(2,128)}, u32[]{:S(2)}) copy-start(s32[1,128,2]{1,2,0:T(2,128)} %param.18) | copy-start | bytes 3076
  7.2 17.8 %copy-start.3 = (bf16[1,128,1536]{2,1,0:T(8,128)(2,1)S(1)}, bf16[1,128,1536]{2,1,0:T(8,128)(2,1)}, u32[]{:S(2)}) copy-start(bf16[1,128,1536]{2,1,0:T(8,128)(2,1)} %param.16) | copy-start | bytes 1179652
  7.2 72.6 %all-gather.3.cloned.1.call-start = ((), (), s32[]{:S(2)}) async-start(), calls=%async_computation.2 | async-start | bytes 1179648 | tf_op jit(solution)/shard_map/all_gather | solution.py:404
  8.8 6.0 %collective-permute-start = (bf16[128,256]{1,0:T(8,128)(2,1)}, bf16[128,256]{1,0:T(8,128)(2,1)S(1)}, u32[]{:S(2)}, u32[]{:S(2)}) collective-permute-start(bf16[128,256]{1,0:T(8,128)(2,1)} %get-tuple-element.20), channel_id=1, source_target_pairs={{0,128},{128,0},{1,129},{129,1},{2,130},{130,2},{3,131},{131,3},{4... | collective-permute-start | bytes 196616 | tf_op jit(solution)/shard_map/ppermute | solution.py:403
  14.8 0.6 copy-start.17
  17.7 1.0 copy-start
  18.7 1.0 copy-start.1
  19.7 1.0 copy-start.2
  20.7 0.8 copy-start.4
  21.8 12.4 %collective-permute-start.2 = (bf16[144,1536]{1,0:T(8,128)(2,1)S(1)}, bf16[144,1536]{1,0:T(8,128)(2,1)S(1)}, u32[]{:S(2)}, u32[]{:S(2)}) collective-permute-start(bf16[144,1536]{1,0:T(8,128)(2,1)S(1)} %get-tuple-element.22), channel_id=1, source_target_pairs={{0,128},{128,0},{1,129},{129,1},{2,130},{130,2},{3,131},{131,3},{4... | collective-permute-start | bytes 1327112 | tf_op jit(solution)/shard_map/ppermute | solution.py:412
  26.7 54.5 %all-to-all-start.1 = ((bf16[8,48,1536]{2,1,0:T(8,128)(2,1)}), bf16[8,48,1536]{2,1,0:T(8,128)(2,1)}, u32[]{:S(2)}, u32[]{:S(2)}) async-start(bf16[8,48,1536]{2,1,0:T(8,128)(2,1)} %route.1), calls=%async_computation.1 | async-start | bytes 2359296 | tf_op jit(solution)/shard_map/all_to_all | solution.py:415
  39.1 22.2 %collective-permute-start.7 = (bf16[4,96,1024]{2,1,0:T(8,128)(2,1)}, bf16[4,96,1024]{2,1,0:T(8,128)(2,1)S(1)}, u32[]{:S(2)}, u32[]{:S(2)}) collective-permute-start(bf16[4,96,1024]{2,1,0:T(8,128)(2,1)} %get-tuple-element.25.refs_10_), channel_id=1, source_target_pairs={{0,4},{2,6},{4,0},{6,2},{1,5},{3,7},{5,1},{7,3},{8,12},{10,14},{12... | collective-permute-start | bytes 2359304 | tf_op jit(solution)/shard_map/ppermute | solution.py:426
  42.3 23.1 %collective-permute-start.4 = (bf16[4,96,1024]{2,1,0:T(8,128)(2,1)}, bf16[4,96,1024]{2,1,0:T(8,128)(2,1)}, u32[]{:S(2)}, u32[]{:S(2)}) collective-permute-start(bf16[4,96,1024]{2,1,0:T(8,128)(2,1)} %get-tuple-element.24), channel_id=1, source_target_pairs={{0,1},{1,0},{2,3},{3,2},{4,5},{5,4},{6,7},{7,6},{8,9},{9,8},{10,11... | collective-permute-start | bytes 2359304 | tf_op jit(solution)/shard_map/ppermute | solution.py:425
  43.8 32.0 %collective-permute-start.6 = (bf16[4,96,1024]{2,1,0:T(8,128)(2,1)}, bf16[4,96,1024]{2,1,0:T(8,128)(2,1)}, u32[]{:S(2)}, u32[]{:S(2)}) collective-permute-start(bf16[4,96,1024]{2,1,0:T(8,128)(2,1)} %get-tuple-element.25.refs_10_), channel_id=1, source_target_pairs={{0,6},{2,0},{4,2},{6,4},{1,7},{3,1},{5,3},{7,5},{8,14},{10,8},{12,... | collective-permute-start | bytes 2359304 | tf_op jit(solution)/shard_map/ppermute | solution.py:426
  44.8 33.6 %collective-permute-start.5 = (bf16[4,96,1024]{2,1,0:T(8,128)(2,1)}, bf16[4,96,1024]{2,1,0:T(8,128)(2,1)}, u32[]{:S(2)}, u32[]{:S(2)}) collective-permute-start(bf16[4,96,1024]{2,1,0:T(8,128)(2,1)} %get-tuple-element.25.refs_10_), channel_id=1, source_target_pairs={{0,2},{2,4},{4,6},{6,0},{1,3},{3,5},{5,7},{7,1},{8,10},{10,12},{12... | collective-permute-start | bytes 2359304 | tf_op jit(solution)/shard_map/ppermute | solution.py:426
  45.8 34.6 %collective-permute-start.1 = (bf16[144,1536]{1,0:T(8,128)(2,1)S(1)}, bf16[144,1536]{1,0:T(8,128)(2,1)S(1)}, u32[]{:S(2)}, u32[]{:S(2)}) collective-permute-start(bf16[144,1536]{1,0:T(8,128)(2,1)S(1)} %get-tuple-element.21.p00), channel_id=1, source_target_pairs={{0,8},{8,0},{1,9},{9,1},{2,10},{10,2},{3,11},{11,3},{4,12},{12,4},... | collective-permute-start | bytes 1327112 | tf_op jit(solution)/shard_map/ppermute | solution.py:431
  61.4 18.4 %copy-start.18 = (bf16[4,96,1024]{2,1,0:T(8,128)(2,1)}, bf16[4,96,1024]{2,1,0:T(8,128)(2,1)S(1)}, u32[]{:S(2)}) copy-start(bf16[4,96,1024]{2,1,0:T(8,128)(2,1)S(1)} %collective-permute-done.7.refs_13_) | copy-start | bytes 2359300
  61.4 21.2 %collective-permute-start.3 = (bf16[144,1536]{1,0:T(8,128)(2,1)S(1)}, bf16[144,1536]{1,0:T(8,128)(2,1)S(1)}, u32[]{:S(2)}, u32[]{:S(2)}) collective-permute-start(bf16[144,1536]{1,0:T(8,128)(2,1)S(1)} %collective-permute-done.2.p10), channel_id=1, source_target_pairs={{0,8},{8,0},{1,9},{9,1},{2,10},{10,2},{3,11},{11,3},{4,12},{12,4},... | collective-permute-start | bytes 1327112 | tf_op jit(solution)/shard_map/ppermute | solution.py:431
  65.4 58.3 %collective-permute-start.19 = (bf16[4,96,1024]{2,1,0:T(8,128)(2,1)}, bf16[4,96,1024]{2,1,0:T(8,128)(2,1)}, u32[]{:S(2)}, u32[]{:S(2)}) collective-permute-start(bf16[4,96,1024]{2,1,0:T(8,128)(2,1)} %collective-permute-done.4.refs_14_), channel_id=1, source_target_pairs={{0,2},{2,4},{4,6},{6,0},{1,3},{3,5},{5,7},{7,1},{8,10},{10,12},{12... | collective-permute-start | bytes 2359304 | tf_op jit(solution)/shard_map/ppermute | solution.py:428
  75.8 48.3 %collective-permute-start.20 = (bf16[4,96,1024]{2,1,0:T(8,128)(2,1)}, bf16[4,96,1024]{2,1,0:T(8,128)(2,1)}, u32[]{:S(2)}, u32[]{:S(2)}) collective-permute-start(bf16[4,96,1024]{2,1,0:T(8,128)(2,1)} %collective-permute-done.4.refs_14_), channel_id=1, source_target_pairs={{0,6},{2,0},{4,2},{6,4},{1,7},{3,1},{5,3},{7,5},{8,14},{10,8},{12,... | collective-permute-start | bytes 2359304 | tf_op jit(solution)/shard_map/ppermute | solution.py:428
  78.4 45.7 %collective-permute-start.21 = (bf16[4,96,1024]{2,1,0:T(8,128)(2,1)}, bf16[4,96,1024]{2,1,0:T(8,128)(2,1)}, u32[]{:S(2)}, u32[]{:S(2)}) collective-permute-start(bf16[4,96,1024]{2,1,0:T(8,128)(2,1)} %collective-permute-done.4.refs_14_), channel_id=1, source_target_pairs={{0,4},{2,6},{4,0},{6,2},{1,5},{3,7},{5,1},{7,3},{8,12},{10,14},{12... | collective-permute-start | bytes 2359304 | tf_op jit(solution)/shard_map/ppermute | solution.py:428
  79.8 4.6 %copy-start.8 = (bf16[16,128,256]{2,1,0:T(8,128)(2,1)S(1)}, bf16[16,128,256]{2,1,0:T(8,128)(2,1)}, u32[]{:S(2)}) copy-start(bf16[16,128,256]{2,1,0:T(8,128)(2,1)} %all-gather.3.cloned.1.call-done) | copy-start | bytes 3145732
  80.4 0.8 copy-start.9
  81.2 39.9 %collective-permute-start.10 = (bf16[4,96,1536]{2,1,0:T(8,128)(2,1)}, bf16[4,96,1536]{2,1,0:T(8,128)(2,1)}, u32[]{:S(2)}, u32[]{:S(2)}) collective-permute-start(bf16[4,96,1536]{2,1,0:T(8,128)(2,1)} %bitcast.22.refs_0_), channel_id=1, source_target_pairs={{0,1},{1,0},{2,3},{3,2},{4,5},{5,4},{6,7},{7,6},{8,9},{9,8},{10,11... | collective-permute-start | bytes 3538952 | tf_op jit(solution)/shard_map/ppermute | solution.py:417
  82.6 0.8 copy-start.11
  83.4 35.4 %collective-permute-start.11 = (bf16[4,96,1536]{2,1,0:T(8,128)(2,1)}, bf16[4,96,1536]{2,1,0:T(8,128)(2,1)}, u32[]{:S(2)}, u32[]{:S(2)}) collective-permute-start(bf16[4,96,1536]{2,1,0:T(8,128)(2,1)} %bitcast.22.refs_0_), channel_id=1, source_target_pairs={{0,16},{16,0},{1,17},{17,1},{2,18},{18,2},{3,19},{19,3},{4,20},{20... | collective-permute-start | bytes 3538952 | tf_op jit(solution)/shard_map/ppermute | solution.py:418
  84.4 1.0 copy-start.10
  85.4 1.0 copy-start.12
  86.4 0.7 copy-start.15
  99.7 0.7 copy-start.13
  100.4 18.4 %copy-start.14 = (bf16[2,128,768]{2,1,0:T(8,128)(2,1)S(1)}, bf16[2,128,768]{2,1,0:T(8,128)(2,1)}, u32[]{:S(2)}) copy-start(bf16[2,128,768]{2,1,0:T(8,128)(2,1)} %copy-done.13) | copy-start | bytes 1179652
  100.4 52.6 %all-to-all-start = ((bf16[8,2,128,256]{3,2,1,0:T(8,128)(2,1)}), bf16[8,2,128,256]{3,2,1,0:T(8,128)(2,1)S(1)}, u32[]{:S(2)}, u32[]{:S(2)}) async-start(bf16[8,2,128,256]{3,2,1,0:T(8,128)(2,1)} %get-tuple-element.26), calls=%async_computation | async-start | bytes 2097152 | tf_op jit(solution)/shard_map/all_to_all | solution.py:437
  118.8 5.4 %collective-permute-start.8 = (bf16[2,128,768]{2,1,0:T(8,128)(2,1)S(1)}, bf16[2,128,768]{2,1,0:T(8,128)(2,1)S(1)}, u32[]{:S(2)}, u32[]{:S(2)}) collective-permute-start(bf16[2,128,768]{2,1,0:T(8,128)(2,1)S(1)} %copy-done.14), channel_id=1, source_target_pairs={{0,8},{8,0},{1,9},{9,1},{2,10},{10,2},{3,11},{11,3},{4,12},{12,4},... | collective-permute-start | bytes 1179656 | tf_op jit(solution)/shard_map/ppermute | solution.py:436
  121.0 32.9 %collective-permute-start.14 = (bf16[4,96,1536]{2,1,0:T(8,128)(2,1)}, bf16[4,96,1536]{2,1,0:T(8,128)(2,1)}, u32[]{:S(2)}, u32[]{:S(2)}) collective-permute-start(bf16[4,96,1536]{2,1,0:T(8,128)(2,1)} %bitcast.22.refs_0_), channel_id=1, source_target_pairs={{0,8},{8,0},{1,9},{9,1},{2,10},{10,2},{3,11},{11,3},{4,12},{12,4},... | collective-permute-start | bytes 3538952 | tf_op jit(solution)/shard_map/ppermute | solution.py:421
  123.6 15.6 %collective-permute-start.12 = (bf16[2,96,1536]{2,1,0:T(8,128)(2,1)}, bf16[2,96,1536]{2,1,0:T(8,128)(2,1)}, u32[]{:S(2)}, u32[]{:S(2)}) collective-permute-start(bf16[2,96,1536]{2,1,0:T(8,128)(2,1)} %half.2), channel_id=1, source_target_pairs={{0,1},{1,0},{2,3},{3,2},{4,5},{5,4},{6,7},{7,6},{8,9},{9,8},{10,11... | collective-permute-start | bytes 1769480 | tf_op jit(solution)/shard_map/ppermute | solution.py:419
  124.0 28.3 %collective-permute-start.13 = (bf16[2,96,1536]{2,1,0:T(8,128)(2,1)}, bf16[2,96,1536]{2,1,0:T(8,128)(2,1)}, u32[]{:S(2)}, u32[]{:S(2)}) collective-permute-start(bf16[2,96,1536]{2,1,0:T(8,128)(2,1)} %half.3), channel_id=1, source_target_pairs={{0,16},{16,0},{1,17},{17,1},{2,18},{18,2},{3,19},{19,3},{4,20},{20... | collective-permute-start | bytes 1769480 | tf_op jit(solution)/shard_map/ppermute | solution.py:419
  124.1 32.1 %collective-permute-start.15 = (bf16[4,96,1536]{2,1,0:T(8,128)(2,1)}, bf16[4,96,1536]{2,1,0:T(8,128)(2,1)}, u32[]{:S(2)}, u32[]{:S(2)}) collective-permute-start(bf16[4,96,1536]{2,1,0:T(8,128)(2,1)} %collective-permute-done.10.rows_ref.refs_1_), channel_id=1, source_target_pairs={{0,8},{8,0},{1,9},{9,1},{2,10},{10,2},{3,11},{11,3},{4,12},{12,4},... | collective-permute-start | bytes 3538952 | tf_op jit(solution)/shard_map/ppermute | solution.py:421
  124.2 32.0 %collective-permute-start.16 = (bf16[4,96,1536]{2,1,0:T(8,128)(2,1)}, bf16[4,96,1536]{2,1,0:T(8,128)(2,1)S(1)}, u32[]{:S(2)}, u32[]{:S(2)}) collective-permute-start(bf16[4,96,1536]{2,1,0:T(8,128)(2,1)} %collective-permute-done.11.rows_ref.refs_2_), channel_id=1, source_target_pairs={{0,8},{8,0},{1,9},{9,1},{2,10},{10,2},{3,11},{11,3},{4,12},{12,4},... | collective-permute-start | bytes 3538952 | tf_op jit(solution)/shard_map/ppermute | solution.py:421
  139.2 17.0 %collective-permute-start.17 = (bf16[2,96,1536]{2,1,0:T(8,128)(2,1)}, bf16[2,96,1536]{2,1,0:T(8,128)(2,1)}, u32[]{:S(2)}, u32[]{:S(2)}) collective-permute-start(bf16[2,96,1536]{2,1,0:T(8,128)(2,1)} %collective-permute-done.12.refs_3_), channel_id=1, source_target_pairs={{0,8},{8,0},{1,9},{9,1},{2,10},{10,2},{3,11},{11,3},{4,12},{12,4},... | collective-permute-start | bytes 1769480 | tf_op jit(solution)/shard_map/ppermute | solution.py:421
  152.4 3.8 %collective-permute-start.18 = (bf16[2,96,1536]{2,1,0:T(8,128)(2,1)}, bf16[2,96,1536]{2,1,0:T(8,128)(2,1)}, u32[]{:S(2)}, u32[]{:S(2)}) collective-permute-start(bf16[2,96,1536]{2,1,0:T(8,128)(2,1)} %collective-permute-done.13.refs_4_), channel_id=1, source_target_pairs={{0,8},{8,0},{1,9},{9,1},{2,10},{10,2},{3,11},{11,3},{4,12},{12,4},... | collective-permute-start | bytes 1769480 | tf_op jit(solution)/shard_map/ppermute | solution.py:421
  153.2 0.7 copy-start.5
  153.9 20.0 %collective-permute-start.9 = (bf16[128,1024]{1,0:T(8,128)(2,1)S(1)}, bf16[128,1024]{1,0:T(8,128)(2,1)S(1)}, u32[]{:S(2)}, u32[]{:S(2)}) collective-permute-start(bf16[128,1024]{1,0:T(8,128)(2,1)S(1)} %get-tuple-element.30), channel_id=1, source_target_pairs={{0,128},{128,0},{1,129},{129,1},{2,130},{130,2},{3,131},{131,3},{4... | collective-permute-start | bytes 786440 | tf_op jit(solution)/shard_map/ppermute | solution.py:442
  156.2 1.0 copy-start.19
  174.0 0.7 copy-start.16
Sparse Core Ops, SparseCore 0:
  17.1 52.2 all-gather.2

commit v3 on v2

--- a/solution.py
+++ b/solution.py
@@ -15,13 +15,13 @@
 SCALE = HEAD_DIM ** (-0.5)
 LOG2E = 1.4426950408889634
 SWAP = [(0, 1), (1, 0)]
-RIGHT = [(i, (i + 1) % 4) for i in range(4)]
-LEFT = [(i, (i - 1) % 4) for i in range(4)]
-ACROSS = [(i, (i + 2) % 4) for i in range(4)]
 Z = ("zq", "zl")
 HALF = MEMBERS * HEAD_DIM
 F32 = jnp.float32
 BF16 = jnp.bfloat16
+
+
+ANY = pl.BlockSpec(memory_space=pl.ANY)
 
 
 def vmem_specs(count):
@@ -107,6 +107,23 @@
         out_specs=(block, block),
         name="halves",
     )(dp[None], hidden, after)
+
+
+def beside_kernel(keep_ref, other_ref, _, out_ref):
+    out_ref[0] = keep_ref[...]
+    out_ref[1] = other_ref[...]
+
+
+def beside(keep, other, after):
+    block = pl.BlockSpec((1,) + keep.shape[1:], lambda m: (m, 0, 0))
+    return pl.pallas_call(
+        beside_kernel,
+        grid=keep.shape[:1],
+        out_shape=jax.ShapeDtypeStruct((2,) + keep.shape, keep.dtype),
+        in_specs=[block, block, ANY],
+        out_specs=pl.BlockSpec((2, 1) + keep.shape[1:], lambda m: (0, m, 0, 0)),
+        name="beside",
+    )(keep, other, after)
 
 
 def pack_kernel(
@@ -247,9 +264,8 @@
     )(place, kv, *packs, *after)
 
 
-ANY = pl.BlockSpec(memory_space=pl.ANY)
 HALF_COST = 6
-KV_COST = 10
+KV_COST = 3
 
 
 def joined_kernel(keep_ref, other_ref, out_ref):
@@ -274,7 +290,7 @@
 def mark(after, cost):
     return pl.pallas_call(
         mark_kernel,
-        out_shape=jax.ShapeDtypeStruct((8, HEAD_DIM), F32),
+        out_shape=jax.ShapeDtypeStruct((16, HEAD_DIM), BF16),
         in_specs=[ANY],
         out_specs=vmem_specs(1)[0],
         cost_estimate=pl.CostEstimate(
@@ -303,16 +319,14 @@
 
 
 def down_kernel(shards, place_ref, *refs):
-    hidden, (out_ref, gathered_ref) = (refs[-10:-6], refs[-6:-2]), refs[-2:]
-    routed = refs[:-10]
-    tp, zl, co = (place_ref[i] for i in range(3))
+    routed, (hidden_ref, out_ref, gathered_ref) = refs[:-3], refs[-3:]
+    zl, co = place_ref[0], place_ref[1]
 
     @pl.when(pl.program_id(0) == 0)
     def _():
         for n, (other_seq, other_z, other_core) in enumerate(shards):
             m = 2 * (1 - zl if other_z else zl) + (1 - co if other_core else co)
-            for piece, step in zip(hidden[other_seq], (0, 3, 1, 2)):
-                gathered_ref[n, lax.rem(tp + step, 4)] = piece[m]
+            gathered_ref[n] = hidden_ref[:, other_seq, m]
 
     left_side = gathered_ref[...].reshape(len(shards) * 384, gathered_ref.shape[3])
     right_side = jnp.concatenate([r[...].reshape(-1, out_ref.shape[1]) for r in routed], axis=0)
@@ -321,15 +335,15 @@
 
 def down(place, shards, routed, hidden, tile=512):
     width = routed[0].shape[-1]
-    rows = hidden[0].shape[-1]
-    whole = pl.BlockSpec((4, 96, rows), lambda i, p: (0, 0, 0), pipeline_mode=pl.Buffered(1))
+    rows = hidden.shape[-1]
+    whole = lambda i, p: (0, 0, 0, 0, 0)
     return pl.pallas_call(
         functools.partial(down_kernel, shards),
         grid_spec=pltpu.PrefetchScalarGridSpec(
             num_scalar_prefetch=1,
             grid=(width // tile,),
             in_specs=[pl.BlockSpec(r.shape[:2] + (tile,), lambda i, p: (0, 0, i)) for r in routed]
-            + [whole] * 8,
+            + [pl.BlockSpec(hidden.shape, whole, pipeline_mode=pl.Buffered(1))],
             out_specs=pl.BlockSpec((rows, tile), lambda i, p: (0, i)),
             scratch_shapes=[pltpu.VMEM((len(shards), 4, 96, rows), BF16)],
         ),
@@ -339,7 +353,7 @@
         ),
         compiler_params=pltpu.CompilerParams(vmem_limit_bytes=56 << 20),
         name="down",
-    )(place, *routed, *hidden)
+    )(place, *routed, hidden)
 
 
 def finish_kernel(parts_ref, kept_ref, near_ref, mine_ref, send_ref):
@@ -421,24 +435,21 @@
     shards += tuple(lax.ppermute(rows, "co", SWAP) for rows in shards)
 
     hidden = hidden_act[0].reshape(2, 4, CAPACITY, 2048)
-    hidden, hidden_send = halves(dp, hidden, corner([across[None]]) + corner([outgoing]))
-    hidden_other = lax.ppermute(hidden_send, "dp", SWAP)
-    own = [hidden] + [lax.ppermute(hidden, "tp", move) for move in (RIGHT, LEFT, ACROSS)]
-    other = [hidden_other] + [
-        lax.ppermute(hidden_other, "tp", move) for move in (RIGHT, LEFT, ACROSS)
-    ]
+    reached = corner([routed, mark(kv_all, KV_COST)[None]])
+    keep_half, send_half = halves(dp, hidden, corner([across[None]]) + corner([outgoing]))
+    hidden = beside(keep_half, lax.ppermute(send_half, "dp", SWAP), reached)
+    hidden = lax.all_gather(hidden, "tp", axis=0)
 
     packs = (keep, lax.ppermute(keep, "co", SWAP), across, lax.ppermute(across, "co", SWAP))
-    early = corner([hidden_other] + own[1:])
     dkv, dq_keep, dq_send = attention(
-        jnp.stack([xh, z, co]), kv_all, packs, [early, mark(kv_all, KV_COST)]
+        jnp.stack([xh, z, co]), kv_all, packs, [reached]
     )
     dq_near = lax.ppermute(dq_send, "co", SWAP)
     dkv = lax.all_to_all(dkv, Z, 0, 0, tiled=True)
     mine, send = finish(dkv, dq_keep, dq_near)
 
     names = tuple((seq, z, core) for core in (0, 1) for seq, z in ((0, 0), (1, 0), (0, 1), (1, 1)))
-    down_grad = down(jnp.stack([tp, zl, co]), names, shards, own + other)
+    down_grad = down(jnp.stack([zl, co]), names, shards, hidden)
     grads = spread(xh, mine, lax.ppermute(send, "xh", SWAP), down_grad)
     return tuple(grad[None] for grad in grads) + (down_grad,)
 

time: 187 us -> 187 us (level)
  starting transfers between devices: 48.6 us -> 40.6 us
  waiting for transfers between devices: 60.4 us -> 67.1 us
  Pallas kernels: 44.9 us -> 48.6 us
  local copies, waits for them, and re-layouts: 12.6 us -> 10.1 us
    ppermute x7 -> x1, waiting for transfers between devices: 29.7 us -> 1.82 us  [local(): hidden = beside(keep_half, lax.ppermute(send_half, 'dp', SWAP), reached)]
    ppermute x1, waiting for transfers between devices: 0.01 us -> 13.8 us  [local(): across = lax.ppermute(send, 'xh', SWAP)]
    all_gather x1, waiting for transfers between devices: 0.01 us -> 12.2 us  [local(): kv_all = lax.all_gather(kv, Z, axis=0)]
    ppermute x7 -> x1, starting transfers between devices: 10.2 us -> 0.57 us  [local(): hidden = beside(keep_half, lax.ppermute(send_half, 'dp', SWAP), reached)]
    all_to_all x1, waiting for transfers between devices: 0.01 us -> 5.18 us  [local(): routed = lax.all_to_all(outgoing, ('xh', 'zq'), 0, 0, tiled=True)]
    ppermute x1, waiting for transfers between devices: 13.2 us -> 18.1 us  [local(): lax.ppermute(half(by_x, 2), 'zl', SWAP)]
    pallas_call x1 -> x2, Pallas kernels: 0.6 us -> 4.22 us  [the longest x1 3.62 us: beside(): pl.pallas_call(beside_kernel, grid=keep.shape[:1], out_shape=jax.ShapeDty...]
    unnamed x41 -> x39, local copies, waits for them, and re-layouts: 12.6 us -> 10.1 us
  transfers between devices with their start and end apart: 25 -> 20, of which waited for: 6 -> 8; matrix products, arithmetic and copies ran while one was open for 2% -> 2% of each run, Pallas kernels for 22% -> 22%
where the time goes in v3:
time: 187 us; the launch traced here: 184 us
  waiting for transfers between devices  67.1 us (36%)
  Pallas kernels  48.6 us (26%)
  starting transfers between devices  40.6 us (22%)
  between operations  14.2 us (8%)
  local copies, waits for them, and re-layouts  10.1 us (5%)
  other arithmetic  3.22 us (2%)
    all_to_all x1, starting transfers between devices, local(): dkv = lax.all_to_all(dkv, Z, 0, 0, tiled=True)  18.3 us
    ppermute x1, waiting for transfers between devices, local(): lax.ppermute(half(by_x, 2), 'zl', SWAP)  18.1 us
    pallas_call x1, Pallas kernels, down(): pl.pallas_call(functools.partial(down_kernel, shards), grid_spec=pltpu.Pr...  16.8 us
    ppermute x1, waiting for transfers between devices, local(): across = lax.ppermute(send, 'xh', SWAP)  13.8 us
    pallas_call x1, Pallas kernels, attention(): pl.pallas_call(attention_kernel, out_shape=(jax.ShapeDtypeStruct((8, 2, T...  12.6 us
    all_gather x1, waiting for transfers between devices, local(): kv_all = lax.all_gather(kv, Z, axis=0)  12.2 us
    ppermute x1, waiting for transfers between devices, local(): lax.ppermute(half(by_z, 0), 'dp', SWAP)  12.1 us
    unnamed x39, local copies, waits for them, and re-layouts  10.1 us
  transfers between devices with their start and end apart: 20, of which 8 were waited for; matrix products, arithmetic and copies ran while one was open for 2% of the time, Pallas kernels for 22%

profile of v3, /device:TPU:32, one launch (start us, length us, event | category | flops | bytes accessed | tf_op | source)
XLA Modules:
  0.0 183.9 jit_solution(8506046356112112558)
XLA Ops:
  7.2 0.0 all-gather.5.cloned.1.call-start
  7.2 1.6 pair.1
  8.8 3.0 %collective-permute-start = (bf16[128,256]{1,0:T(8,128)(2,1)}, bf16[128,256]{1,0:T(8,128)(2,1)S(1)}, u32[]{:S(2)}, u32[]{:S(2)}) collective-permute-start(bf16[128,256]{1,0:T(8,128)(2,1)} %get-tuple-element.20), channel_id=1, source_target_pairs={{0,128},{128,0},{1,129},{129,1},{2,130},{130,2},{3,131},{131,3},{4... | collective-permute-start | bytes 196616 | tf_op jit(solution)/shard_map/ppermute | solution.py:417
  11.9 3.0 %collective-permute-done.other_ref = bf16[128,256]{1,0:T(8,128)(2,1)S(1)} collective-permute-done((bf16[128,256]{1,0:T(8,128)(2,1)}, bf16[128,256]{1,0:T(8,128)(2,1)S(1)}, u32[]{:S(2)}, u32[]{:S(2)}) %collective-permute-start) | collective-permute-done | bytes 65568 | tf_op jit(solution)/shard_map/ppermute | solution.py:417
  14.8 0.6 copy-done.17
  15.5 1.5 joined.1
  17.0 0.0 all-gather.5.cloned.1.call-update
  17.0 0.7 copy.16
  17.7 1.0 copy-done
  18.7 1.0 copy-done.1
  19.7 1.0 copy-done.2
  20.7 0.8 copy-done.4
  21.6 0.3 pack.1
  21.9 1.7 route.1
  23.6 10.0 %all-to-all-start = ((bf16[8,48,1536]{2,1,0:T(8,128)(2,1)}), bf16[8,48,1536]{2,1,0:T(8,128)(2,1)S(1)}, u32[]{:S(2)}, u32[]{:S(2)}) async-start(bf16[8,48,1536]{2,1,0:T(8,128)(2,1)} %route.1), calls=%async_computation | async-start | bytes 2359296 | tf_op jit(solution)/shard_map/all_to_all | solution.py:429
  33.6 0.0 all-gather.7.cloned.1.call-start
  33.7 3.5 %collective-permute-start.2 = (bf16[144,1536]{1,0:T(8,128)(2,1)S(1)}, bf16[144,1536]{1,0:T(8,128)(2,1)S(1)}, u32[]{:S(2)}, u32[]{:S(2)}) collective-permute-start(bf16[144,1536]{1,0:T(8,128)(2,1)S(1)} %get-tuple-element.22), channel_id=1, source_target_pairs={{0,128},{128,0},{1,129},{129,1},{2,130},{130,2},{3,131},{131,3},{4... | collective-permute-start | bytes 1327112 | tf_op jit(solution)/shard_map/ppermute | solution.py:426
  37.1 13.8 %collective-permute-done.2.p10 = bf16[144,1536]{1,0:T(8,128)(2,1)S(1)} collective-permute-done((bf16[144,1536]{1,0:T(8,128)(2,1)S(1)}, bf16[144,1536]{1,0:T(8,128)(2,1)S(1)}, u32[]{:S(2)}, u32[]{:S(2)}) %collective-permute-start.2) | collective-permute-done | bytes 442400 | tf_op jit(solution)/shard_map/ppermute | solution.py:426
  51.0 1.3 fusion._
  52.3 3.6 %halves.1 = (bf16[4,96,1024]{2,1,0:T(8,128)(2,1)}, bf16[4,96,1024]{2,1,0:T(8,128)(2,1)}) custom-call(s32[1]{0:T(128)} %bitcast.18.place_ref, bf16[2,4,48,2048]{3,2,1,0:T(8,128)(2,1)} %bitcast.45, bf16[16,128]{1,0:T(8,128)(2,1)} %fusion._), custom_call_target="tpu_custom_call" | custom-call | tf_op jit(solution)/shard_map/halves/pallas_call | solution.py:98
  55.9 0.6 collective-permute-start.15
  56.5 12.2 %all-gather.5.cloned.1.call-done = bf16[16,128,256]{2,1,0:T(8,128)(2,1)} async-done(((bf16[2,128,256]{2,1,0:T(8,128)(2,1)}), bf16[16,128,256]{2,1,0:T(8,128)(2,1)}) %all-gather.5.cloned.1.call-update) | async-done | bytes 1048592 | tf_op jit(solution)/shard_map/all_gather | solution.py:418
  68.7 0.6 mark.1
  69.3 5.2 %all-to-all-done = bf16[8,48,1536]{2,1,0:T(8,128)(2,1)S(1)} async-done(((bf16[8,48,1536]{2,1,0:T(8,128)(2,1)}), bf16[8,48,1536]{2,1,0:T(8,128)(2,1)S(1)}, u32[]{:S(2)}, u32[]{:S(2)}) %all-to-all-start) | async-done | bytes 1179680 | tf_op jit(solution)/shard_map/all_to_all | solution.py:429
  74.4 1.3 fusion.1.refs_0_._
  75.7 1.8 collective-permute-done.15.other_ref
  77.5 0.9 copy-done.15
  78.5 3.6 %beside.1 = bf16[2,4,96,1024]{3,2,1,0:T(8,128)(2,1)} custom-call(bf16[4,96,1024]{2,1,0:T(8,128)(2,1)} %get-tuple-element.29.keep_ref, bf16[4,96,1024]{2,1,0:T(8,128)(2,1)} %copy-done.15, bf16[16,128]{1,0:T(8,128)(2,1)} %fusion.1.refs_0_._), custom_call_target="tpu_custom_call" | custom-call | tf_op jit(solution)/shard_map/beside/pallas_call | solution.py:119
  82.1 0.0 all-gather.7.cloned.1.call-update
  82.1 0.1 collective-permute-start.1
  82.2 0.5 collective-permute-start.3
  82.7 0.1 pad_add_fusion.place_ref
  82.8 0.1 collective-permute-start.10
  82.9 0.0 collective-permute-start.7
  82.9 1.4 collective-permute-start.6
  84.4 0.0 collective-permute-done.1.p01
  84.4 0.9 collective-permute-done.3.p11
  85.3 0.8 copy-done.10
  86.1 1.0 copy-done.11
  87.1 12.6 %attention.1 = (bf16[8,2,128,256]{3,2,1,0:T(8,128)(2,1)}, f32[2,128,768]{2,1,0:T(8,128)S(1)}, bf16[2,128,768]{2,1,0:T(8,128)(2,1)S(1)}) custom-call(s32[3]{0:T(128)S(1)} %pad_add_fusion.place_ref, bf16[8,2,128,256]{3,2,1,0:T(8,128)(2,1)S(1)} %bitcast.44, bf16[144,1536]{1,0:T(8,128)(2,1)S(1)} %get-tuple-element.21.p00, ...), custom_call_target="tpu_custom_call" | custom-call | flops 16000000000 | bytes 8000000 | tf_op jit(solution)/shard_map/attention/pallas_call | solution.py:238
  99.7 0.7 copy-done.12
  100.4 18.3 %all-to-all-start.1 = ((bf16[8,2,128,256]{3,2,1,0:T(8,128)(2,1)}), bf16[8,2,128,256]{3,2,1,0:T(8,128)(2,1)S(1)}, u32[]{:S(2)}, u32[]{:S(2)}) async-start(bf16[8,2,128,256]{3,2,1,0:T(8,128)(2,1)} %get-tuple-element.24), calls=%async_computation.1 | async-start | bytes 2097152 | tf_op jit(solution)/shard_map/all_to_all | solution.py:448
  118.7 0.0 collective-permute-start.4
  118.7 0.0 collective-permute-done.7.rows_ref.refs_2_
  118.7 2.1 %half.2 = bf16[2,96,1536]{2,1,0:T(8,128)(2,1)} custom-call(bf16[4,96,1536]{2,1,0:T(8,128)(2,1)} %collective-permute-done.7.rows_ref.refs_2_), custom_call_target="tpu_custom_call" | custom-call | flops 6000000000 | bytes 2000000 | tf_op jit(solution)/shard_map/half/pallas_call | solution.py:309
  120.8 1.1 collective-permute-start.8
  122.0 2.1 %half.3 = bf16[2,96,1536]{2,1,0:T(8,128)(2,1)} custom-call(bf16[4,96,1536]{2,1,0:T(8,128)(2,1)} %collective-permute-done.6.rows_ref.refs_1_), custom_call_target="tpu_custom_call" | custom-call | flops 6000000000 | bytes 2000000 | tf_op jit(solution)/shard_map/half/pallas_call | solution.py:309
  124.1 0.1 collective-permute-start.9
  124.2 0.1 collective-permute-start.12
  124.4 0.0 collective-permute-done.4.near_ref
  124.4 0.4 collective-permute-start.11
  124.8 12.1 %collective-permute-done.8.refs_3_ = bf16[2,96,1536]{2,1,0:T(8,128)(2,1)S(1)} collective-permute-done((bf16[2,96,1536]{2,1,0:T(8,128)(2,1)}, bf16[2,96,1536]{2,1,0:T(8,128)(2,1)S(1)}, u32[]{:S(2)}, u32[]{:S(2)}) %collective-permute-start.8) | collective-permute-done | bytes 589856 | tf_op jit(solution)/shard_map/ppermute | solution.py:433
  136.8 0.0 collective-permute-start.13
  136.8 18.1 %collective-permute-done.9.refs_4_ = bf16[2,96,1536]{2,1,0:T(8,128)(2,1)} collective-permute-done((bf16[2,96,1536]{2,1,0:T(8,128)(2,1)}, bf16[2,96,1536]{2,1,0:T(8,128)(2,1)}, u32[]{:S(2)}, u32[]{:S(2)}) %collective-permute-start.9) | collective-permute-done | bytes 589856 | tf_op jit(solution)/shard_map/ppermute | solution.py:433
  154.9 0.6 pad_add_fusion.1.place_ref
  155.5 0.0 all-to-all-done.1.parts_ref
  155.5 0.2 finish.1
  155.7 0.7 copy-done.5
  156.4 1.3 collective-permute-start.5
  157.7 0.0 collective-permute-done.12.refs_7_
  157.7 0.0 all-gather.7.cloned.1.call-done
  157.7 16.8 %down.1._ = bf16[1024,1536]{1,0:T(8,128)(2,1)} custom-call(s32[2]{0:T(128)} %pad_add_fusion.1.place_ref, bf16[4,96,1536]{2,1,0:T(8,128)(2,1)} %bitcast.50, bf16[4,96,1536]{2,1,0:T(8,128)(2,1)} %collective-permute-done.6.rows_ref.refs_1_, bf16[4,96,1536]{2,1,0:T(8,128)(2,1)} %collective-permute-done.7.rows_ref.refs_2_, bf16[2,96,1536]{2,1,0:T(8,128)(2,1)} %copy-done.18, ...), custom_call_target="tpu_custom_call" | custom-call | flops 16000000000 | bytes 20000000 | tf_op jit(solution)/shard_map/down/pallas_call | solution.py:340
  174.5 0.7 copy-done.16
  175.2 1.8 %spread.1 = (bf16[128,1536]{1,0:T(8,128)(2,1)}, bf16[128,256]{1,0:T(8,128)(2,1)}, bf16[128,256]{1,0:T(8,128)(2,1)}) custom-call(s32[1]{0:T(128)} %bitcast.place_ref, bf16[128,1024]{1,0:T(8,128)(2,1)} %copy-done.5, bf16[128,1024]{1,0:T(8,128)(2,1)} %copy-done.16, bf16[1024,1536]{1,0:T(8,128)(2,1)} %down.1._), custom_call_target="tpu_custom_call" | custom-call | tf_op jit(solution)/shard_map/spread/pallas_call | solution.py:392
  (36 shorter events, 0.1 us)
Async XLA Ops:
  7.2 14.7 %copy-start.8 = (s32[1,128,2]{1,2,0:T(2,128)S(1)}, s32[1,128,2]{1,2,0:T(2,128)}, u32[]{:S(2)}) copy-start(s32[1,128,2]{1,2,0:T(2,128)} %param.18) | copy-start | bytes 3076
  7.2 14.7 %copy-start.7 = (s32[1,128,2]{1,2,0:T(2,128)S(1)}, s32[1,128,2]{1,2,0:T(2,128)}, u32[]{:S(2)}) copy-start(s32[1,128,2]{1,2,0:T(2,128)} %param.17) | copy-start | bytes 3076
  7.2 14.7 %copy-start.3 = (bf16[1,128,1536]{2,1,0:T(8,128)(2,1)S(1)}, bf16[1,128,1536]{2,1,0:T(8,128)(2,1)}, u32[]{:S(2)}) copy-start(bf16[1,128,1536]{2,1,0:T(8,128)(2,1)} %param.16) | copy-start | bytes 1179652
  7.2 61.5 %all-gather.5.cloned.1.call-start = ((), (), s32[]{:S(2)}) async-start(), calls=%async_computation.2 | async-start | bytes 1179648 | tf_op jit(solution)/shard_map/all_gather | solution.py:418
  8.8 6.0 %collective-permute-start = (bf16[128,256]{1,0:T(8,128)(2,1)}, bf16[128,256]{1,0:T(8,128)(2,1)S(1)}, u32[]{:S(2)}, u32[]{:S(2)}) collective-permute-start(bf16[128,256]{1,0:T(8,128)(2,1)} %get-tuple-element.20), channel_id=1, source_target_pairs={{0,128},{128,0},{1,129},{129,1},{2,130},{130,2},{3,131},{131,3},{4... | collective-permute-start | bytes 196616 | tf_op jit(solution)/shard_map/ppermute | solution.py:417
  14.8 0.6 copy-start.17
  17.7 1.0 copy-start
  18.7 1.0 copy-start.1
  19.7 1.0 copy-start.2
  20.7 0.8 copy-start.4
  23.6 50.9 %all-to-all-start = ((bf16[8,48,1536]{2,1,0:T(8,128)(2,1)}), bf16[8,48,1536]{2,1,0:T(8,128)(2,1)S(1)}, u32[]{:S(2)}, u32[]{:S(2)}) async-start(bf16[8,48,1536]{2,1,0:T(8,128)(2,1)} %route.1), calls=%async_computation | async-start | bytes 2359296 | tf_op jit(solution)/shard_map/all_to_all | solution.py:429
  33.6 124.1 %all-gather.7.cloned.1.call-start = ((), (), s32[]{:S(2)}) async-start(), calls=%async_computation.3 | async-start | bytes 7864320 | tf_op jit(solution)/shard_map/all_gather | solution.py:441
  33.7 17.3 %collective-permute-start.2 = (bf16[144,1536]{1,0:T(8,128)(2,1)S(1)}, bf16[144,1536]{1,0:T(8,128)(2,1)S(1)}, u32[]{:S(2)}, u32[]{:S(2)}) collective-permute-start(bf16[144,1536]{1,0:T(8,128)(2,1)S(1)} %get-tuple-element.22), channel_id=1, source_target_pairs={{0,128},{128,0},{1,129},{129,1},{2,130},{130,2},{3,131},{131,3},{4... | collective-permute-start | bytes 1327112 | tf_op jit(solution)/shard_map/ppermute | solution.py:426
  55.9 21.7 %collective-permute-start.15 = (bf16[4,96,1024]{2,1,0:T(8,128)(2,1)}, bf16[4,96,1024]{2,1,0:T(8,128)(2,1)S(1)}, u32[]{:S(2)}, u32[]{:S(2)}) collective-permute-start(bf16[4,96,1024]{2,1,0:T(8,128)(2,1)} %get-tuple-element.30), channel_id=1, source_target_pairs={{0,1},{1,0},{2,3},{3,2},{4,5},{5,4},{6,7},{7,6},{8,9},{9,8},{10,11... | collective-permute-start | bytes 2359304 | tf_op jit(solution)/shard_map/ppermute | solution.py:440
  74.4 3.1 %copy-start.14 = (bf16[8,48,1536]{2,1,0:T(8,128)(2,1)}, bf16[8,48,1536]{2,1,0:T(8,128)(2,1)S(1)}, u32[]{:S(2)}) copy-start(bf16[8,48,1536]{2,1,0:T(8,128)(2,1)S(1)} %all-to-all-done) | copy-start | bytes 3538948
  77.5 0.9 copy-start.15
  82.1 4.0 %copy-start.6 = (bf16[16,128]{1,0:T(8,128)(2,1)S(1)}, bf16[16,128]{1,0:T(8,128)(2,1)}, u32[]{:S(2)}) copy-start(bf16[16,128]{1,0:T(8,128)(2,1)} %fusion.1.refs_0_._) | copy-start | bytes 12292
  82.1 4.0 %copy-start.9 = (bf16[16,128,256]{2,1,0:T(8,128)(2,1)S(1)}, bf16[16,128,256]{2,1,0:T(8,128)(2,1)}, u32[]{:S(2)}) copy-start(bf16[16,128,256]{2,1,0:T(8,128)(2,1)} %all-gather.5.cloned.1.call-done) | copy-start | bytes 3145732
  82.1 2.2 %collective-permute-start.1 = (bf16[144,1536]{1,0:T(8,128)(2,1)S(1)}, bf16[144,1536]{1,0:T(8,128)(2,1)S(1)}, u32[]{:S(2)}, u32[]{:S(2)}) collective-permute-start(bf16[144,1536]{1,0:T(8,128)(2,1)S(1)} %get-tuple-element.21.p00), channel_id=1, source_target_pairs={{0,8},{8,0},{1,9},{9,1},{2,10},{10,2},{3,11},{11,3},{4,12},{12,4},... | collective-permute-start | bytes 1327112 | tf_op jit(solution)/shard_map/ppermute | solution.py:443
  82.2 3.0 %collective-permute-start.3 = (bf16[144,1536]{1,0:T(8,128)(2,1)S(1)}, bf16[144,1536]{1,0:T(8,128)(2,1)S(1)}, u32[]{:S(2)}, u32[]{:S(2)}) collective-permute-start(bf16[144,1536]{1,0:T(8,128)(2,1)S(1)} %collective-permute-done.2.p10), channel_id=1, source_target_pairs={{0,8},{8,0},{1,9},{9,1},{2,10},{10,2},{3,11},{11,3},{4,12},{12,4},... | collective-permute-start | bytes 1327112 | tf_op jit(solution)/shard_map/ppermute | solution.py:443
  82.8 73.6 %collective-permute-start.10 = (bf16[4,96,1536]{2,1,0:T(8,128)(2,1)}, bf16[4,96,1536]{2,1,0:T(8,128)(2,1)}, u32[]{:S(2)}, u32[]{:S(2)}) collective-permute-start(bf16[4,96,1536]{2,1,0:T(8,128)(2,1)} %bitcast.47), channel_id=1, source_target_pairs={{0,8},{8,0},{1,9},{9,1},{2,10},{10,2},{3,11},{11,3},{4,12},{12,4},... | collective-permute-start | bytes 3538952 | tf_op jit(solution)/shard_map/ppermute | solution.py:435
  82.9 35.8 %collective-permute-start.7 = (bf16[4,96,1536]{2,1,0:T(8,128)(2,1)}, bf16[4,96,1536]{2,1,0:T(8,128)(2,1)}, u32[]{:S(2)}, u32[]{:S(2)}) collective-permute-start(bf16[4,96,1536]{2,1,0:T(8,128)(2,1)} %bitcast.48), channel_id=1, source_target_pairs={{0,16},{16,0},{1,17},{17,1},{2,18},{18,2},{3,19},{19,3},{4,20},{20... | collective-permute-start | bytes 3538952 | tf_op jit(solution)/shard_map/ppermute | solution.py:432
  82.9 39.0 %collective-permute-start.6 = (bf16[4,96,1536]{2,1,0:T(8,128)(2,1)}, bf16[4,96,1536]{2,1,0:T(8,128)(2,1)}, u32[]{:S(2)}, u32[]{:S(2)}) collective-permute-start(bf16[4,96,1536]{2,1,0:T(8,128)(2,1)} %bitcast.49), channel_id=1, source_target_pairs={{0,1},{1,0},{2,3},{3,2},{4,5},{5,4},{6,7},{7,6},{8,9},{9,8},{10,11... | collective-permute-start | bytes 3538952 | tf_op jit(solution)/shard_map/ppermute | solution.py:431
  85.3 0.8 copy-start.10
  86.1 1.0 copy-start.11
  99.6 0.7 copy-start.12
  100.4 18.3 %copy-start.13 = (bf16[2,128,768]{2,1,0:T(8,128)(2,1)S(1)}, bf16[2,128,768]{2,1,0:T(8,128)(2,1)}, u32[]{:S(2)}) copy-start(bf16[2,128,768]{2,1,0:T(8,128)(2,1)} %copy-done.12) | copy-start | bytes 1179652
  100.4 55.1 %all-to-all-start.1 = ((bf16[8,2,128,256]{3,2,1,0:T(8,128)(2,1)}), bf16[8,2,128,256]{3,2,1,0:T(8,128)(2,1)S(1)}, u32[]{:S(2)}, u32[]{:S(2)}) async-start(bf16[8,2,128,256]{3,2,1,0:T(8,128)(2,1)} %get-tuple-element.24), calls=%async_computation.1 | async-start | bytes 2097152 | tf_op jit(solution)/shard_map/all_to_all | solution.py:448
  118.7 5.7 %collective-permute-start.4 = (bf16[2,128,768]{2,1,0:T(8,128)(2,1)S(1)}, bf16[2,128,768]{2,1,0:T(8,128)(2,1)S(1)}, u32[]{:S(2)}, u32[]{:S(2)}) collective-permute-start(bf16[2,128,768]{2,1,0:T(8,128)(2,1)S(1)} %copy-done.13), channel_id=1, source_target_pairs={{0,8},{8,0},{1,9},{9,1},{2,10},{10,2},{3,11},{11,3},{4,12},{12,4},... | collective-permute-start | bytes 1179656 | tf_op jit(solution)/shard_map/ppermute | solution.py:447
  120.8 16.0 %collective-permute-start.8 = (bf16[2,96,1536]{2,1,0:T(8,128)(2,1)}, bf16[2,96,1536]{2,1,0:T(8,128)(2,1)S(1)}, u32[]{:S(2)}, u32[]{:S(2)}) collective-permute-start(bf16[2,96,1536]{2,1,0:T(8,128)(2,1)} %half.2), channel_id=1, source_target_pairs={{0,1},{1,0},{2,3},{3,2},{4,5},{5,4},{6,7},{7,6},{8,9},{9,8},{10,11... | collective-permute-start | bytes 1769480 | tf_op jit(solution)/shard_map/ppermute | solution.py:433
  124.1 30.8 %collective-permute-start.9 = (bf16[2,96,1536]{2,1,0:T(8,128)(2,1)}, bf16[2,96,1536]{2,1,0:T(8,128)(2,1)}, u32[]{:S(2)}, u32[]{:S(2)}) collective-permute-start(bf16[2,96,1536]{2,1,0:T(8,128)(2,1)} %half.3), channel_id=1, source_target_pairs={{0,16},{16,0},{1,17},{17,1},{2,18},{18,2},{3,19},{19,3},{4,20},{20... | collective-permute-start | bytes 1769480 | tf_op jit(solution)/shard_map/ppermute | solution.py:433
  124.2 33.4 %collective-permute-start.12 = (bf16[4,96,1536]{2,1,0:T(8,128)(2,1)}, bf16[4,96,1536]{2,1,0:T(8,128)(2,1)}, u32[]{:S(2)}, u32[]{:S(2)}) collective-permute-start(bf16[4,96,1536]{2,1,0:T(8,128)(2,1)} %collective-permute-done.7.rows_ref.refs_2_), channel_id=1, source_target_pairs={{0,8},{8,0},{1,9},{9,1},{2,10},{10,2},{3,11},{11,3},{4,12},{12,4},... | collective-permute-start | bytes 3538952 | tf_op jit(solution)/shard_map/ppermute | solution.py:435
  124.4 33.3 %collective-permute-start.11 = (bf16[4,96,1536]{2,1,0:T(8,128)(2,1)}, bf16[4,96,1536]{2,1,0:T(8,128)(2,1)}, u32[]{:S(2)}, u32[]{:S(2)}) collective-permute-start(bf16[4,96,1536]{2,1,0:T(8,128)(2,1)} %collective-permute-done.6.rows_ref.refs_1_), channel_id=1, source_target_pairs={{0,8},{8,0},{1,9},{9,1},{2,10},{10,2},{3,11},{11,3},{4,12},{12,4},... | collective-permute-start | bytes 3538952 | tf_op jit(solution)/shard_map/ppermute | solution.py:435
  136.8 20.9 %copy-start.18 = (bf16[2,96,1536]{2,1,0:T(8,128)(2,1)}, bf16[2,96,1536]{2,1,0:T(8,128)(2,1)S(1)}, u32[]{:S(2)}) copy-start(bf16[2,96,1536]{2,1,0:T(8,128)(2,1)S(1)} %collective-permute-done.8.refs_3_) | copy-start | bytes 1769476
  136.8 20.8 %collective-permute-start.13 = (bf16[2,96,1536]{2,1,0:T(8,128)(2,1)S(1)}, bf16[2,96,1536]{2,1,0:T(8,128)(2,1)}, u32[]{:S(2)}, u32[]{:S(2)}) collective-permute-start(bf16[2,96,1536]{2,1,0:T(8,128)(2,1)S(1)} %collective-permute-done.8.refs_3_), channel_id=1, source_target_pairs={{0,8},{8,0},{1,9},{9,1},{2,10},{10,2},{3,11},{11,3},{4,12},{12,4},... | collective-permute-start | bytes 1769480 | tf_op jit(solution)/shard_map/ppermute | solution.py:435
  154.9 2.8 %collective-permute-start.14 = (bf16[2,96,1536]{2,1,0:T(8,128)(2,1)}, bf16[2,96,1536]{2,1,0:T(8,128)(2,1)}, u32[]{:S(2)}, u32[]{:S(2)}) collective-permute-start(bf16[2,96,1536]{2,1,0:T(8,128)(2,1)} %collective-permute-done.9.refs_4_), channel_id=1, source_target_pairs={{0,8},{8,0},{1,9},{9,1},{2,10},{10,2},{3,11},{11,3},{4,12},{12,4},... | collective-permute-start | bytes 1769480 | tf_op jit(solution)/shard_map/ppermute | solution.py:435
  155.7 0.7 copy-start.5
  156.4 18.1 %collective-permute-start.5 = (bf16[128,1024]{1,0:T(8,128)(2,1)S(1)}, bf16[128,1024]{1,0:T(8,128)(2,1)S(1)}, u32[]{:S(2)}, u32[]{:S(2)}) collective-permute-start(bf16[128,1024]{1,0:T(8,128)(2,1)S(1)} %get-tuple-element.28), channel_id=1, source_target_pairs={{0,128},{128,0},{1,129},{129,1},{2,130},{130,2},{3,131},{131,3},{4... | collective-permute-start | bytes 786440 | tf_op jit(solution)/shard_map/ppermute | solution.py:453
  174.5 0.7 copy-start.16
Sparse Core Ops, SparseCore 0:
  17.1 51.4 all-gather.4
  82.3 70.4 all-gather.6

commit v4 on v3

--- a/solution.py
+++ b/solution.py
@@ -264,7 +264,7 @@
     )(place, kv, *packs, *after)
 
 
-HALF_COST = 6
+PART_COST = 6
 KV_COST = 3
 
 
@@ -300,22 +300,22 @@
     )(after)
 
 
-def half_kernel(first, rows_ref, out_ref):
-    out_ref[...] = rows_ref[first : first + 2]
-
-
-def half(rows, first, cost=HALF_COST):
-    shape = (2,) + rows.shape[1:]
-    return pl.pallas_call(
-        functools.partial(half_kernel, first),
-        out_shape=jax.ShapeDtypeStruct(shape, rows.dtype),
+def part_kernel(rows, rows_ref, out_ref):
+    out_ref[...] = rows_ref[rows]
+
+
+def part(array, rows):
+    shape = (rows.stop - rows.start,) + array.shape[1:]
+    return pl.pallas_call(
+        functools.partial(part_kernel, rows),
+        out_shape=jax.ShapeDtypeStruct(shape, array.dtype),
         in_specs=vmem_specs(1),
         out_specs=vmem_specs(1)[0],
         cost_estimate=pl.CostEstimate(
-            flops=cost * 1_000_000_000, transcendentals=0, bytes_accessed=2_000_000
-        ),
-        name="half",
-    )(rows)
+            flops=PART_COST * 1_000_000_000, transcendentals=0, bytes_accessed=2_000_000
+        ),
+        name="part",
+    )(array)
 
 
 def down_kernel(shards, place_ref, *refs):
@@ -430,13 +430,16 @@
     routed = routed.reshape(4, 2 * CAPACITY, moe_grad.shape[2])
     by_x = lax.ppermute(routed, "dp", SWAP)
     by_z = lax.ppermute(routed, "zl", SWAP)
-    diagonal = (lax.ppermute(half(by_z, 0), "dp", SWAP), lax.ppermute(half(by_x, 2), "zl", SWAP))
+    diagonal = (
+        lax.ppermute(part(by_z, slice(0, 2)), "dp", SWAP),
+        lax.ppermute(part(by_x, slice(2, 4)), "zl", SWAP),
+    )
     shards = (routed, by_x, by_z) + diagonal
     shards += tuple(lax.ppermute(rows, "co", SWAP) for rows in shards)
 
     hidden = hidden_act[0].reshape(2, 4, CAPACITY, 2048)
-    reached = corner([routed, mark(kv_all, KV_COST)[None]])
-    keep_half, send_half = halves(dp, hidden, corner([across[None]]) + corner([outgoing]))
+    reached = corner([routed, mark(kv_all, KV_COST)[None], across[None]])
+    keep_half, send_half = halves(dp, hidden, corner([outgoing]))
     hidden = beside(keep_half, lax.ppermute(send_half, "dp", SWAP), reached)
     hidden = lax.all_gather(hidden, "tp", axis=0)
 

time: 187 us -> 183 us (0.979)
  starting transfers between devices: 40.6 us -> 36.5 us
    all_gather x1, waiting for transfers between devices: 12.2 us -> 25.4 us  [local(): kv_all = lax.all_gather(kv, Z, axis=0)]
    ppermute x1, waiting for transfers between devices: 13.8 us -> 7.74 us  [local(): across = lax.ppermute(send, 'xh', SWAP)]
    all_to_all x1, waiting for transfers between devices: 5.18 us -> 0.01 us  [local(): routed = lax.all_to_all(outgoing, ('xh', 'zq'), 0, 0, tiled=True)]
    all_to_all x1, starting transfers between devices: 18.3 us -> 14 us  [local(): dkv = lax.all_to_all(dkv, Z, 0, 0, tiled=True)]
    ppermute x1, starting transfers between devices: 0.01 us -> 2 us  [local(): by_z = lax.ppermute(routed, 'zl', SWAP)]
  transfers between devices with their start and end apart: 20 -> 20, of which waited for: 8 -> 7; matrix products, arithmetic and copies ran while one was open for 2% -> 2% of each run, Pallas kernels for 22% -> 22%
where the time goes in v4:
time: 183 us; the launch traced here: 180 us
  waiting for transfers between devices  67.3 us (37%)
  Pallas kernels  48.6 us (27%)
  starting transfers between devices  36.5 us (20%)
  between operations  14.2 us (8%)
  local copies, waits for them, and re-layouts  11.3 us (6%)
  other arithmetic  1.94 us (1%)
    all_gather x1, waiting for transfers between devices, local(): kv_all = lax.all_gather(kv, Z, axis=0)  25.4 us
    ppermute x1, waiting for transfers between devices, local(): lax.ppermute(part(by_x, slice(2, 4)), 'zl', SWAP)  18.1 us
    pallas_call x1, Pallas kernels, down(): pl.pallas_call(functools.partial(down_kernel, shards), grid_spec=pltpu.Pr...  16.8 us
    all_to_all x1, starting transfers between devices, local(): dkv = lax.all_to_all(dkv, Z, 0, 0, tiled=True)  14 us
    ppermute x1, waiting for transfers between devices, local(): lax.ppermute(part(by_z, slice(0, 2)), 'dp', SWAP)  12.6 us
    pallas_call x1, Pallas kernels, attention(): pl.pallas_call(attention_kernel, out_shape=(jax.ShapeDtypeStruct((8, 2, T...  12.6 us
    unnamed x39, local copies, waits for them, and re-layouts  10.1 us
    all_to_all x1, starting transfers between devices, local(): routed = lax.all_to_all(outgoing, ('xh', 'zq'), 0, 0, tiled=True)  10 us
  transfers between devices with their start and end apart: 20, of which 7 were waited for; matrix products, arithmetic and copies ran while one was open for 2% of the time, Pallas kernels for 22%

profile of v4, /device:TPU:32, one launch (start us, length us, event | category | flops | bytes accessed | tf_op | source)
XLA Modules:
  0.0 179.9 jit_solution(10904773641198016747)
XLA Ops:
  7.2 0.0 all-gather.5.cloned.1.call-start
  7.2 1.6 pair.1
  8.8 3.0 %collective-permute-start = (bf16[128,256]{1,0:T(8,128)(2,1)}, bf16[128,256]{1,0:T(8,128)(2,1)S(1)}, u32[]{:S(2)}, u32[]{:S(2)}) collective-permute-start(bf16[128,256]{1,0:T(8,128)(2,1)} %get-tuple-element.20), channel_id=1, source_target_pairs={{0,128},{128,0},{1,129},{129,1},{2,130},{130,2},{3,131},{131,3},{4... | collective-permute-start | bytes 196616 | tf_op jit(solution)/shard_map/ppermute | solution.py:417
  11.9 3.0 %collective-permute-done.other_ref = bf16[128,256]{1,0:T(8,128)(2,1)S(1)} collective-permute-done((bf16[128,256]{1,0:T(8,128)(2,1)}, bf16[128,256]{1,0:T(8,128)(2,1)S(1)}, u32[]{:S(2)}, u32[]{:S(2)}) %collective-permute-start) | collective-permute-done | bytes 65568 | tf_op jit(solution)/shard_map/ppermute | solution.py:417
  14.8 0.6 copy-done.17
  15.5 1.5 joined.1
  17.0 0.0 all-gather.5.cloned.1.call-update
  17.0 0.7 copy.16
  17.7 1.0 copy-done
  18.7 1.0 copy-done.1
  19.7 1.0 copy-done.2
  20.7 0.8 copy-done.4
  21.6 0.3 pack.1
  21.9 1.7 route.1
  23.6 10.0 %all-to-all-start = ((bf16[8,48,1536]{2,1,0:T(8,128)(2,1)}), bf16[8,48,1536]{2,1,0:T(8,128)(2,1)S(1)}, u32[]{:S(2)}, u32[]{:S(2)}) async-start(bf16[8,48,1536]{2,1,0:T(8,128)(2,1)} %route.1), calls=%async_computation | async-start | bytes 2359296 | tf_op jit(solution)/shard_map/all_to_all | solution.py:429
  33.6 0.0 all-gather.7.cloned.1.call-start
  33.7 1.3 slice_bitcast_fusion._
  34.9 3.6 %halves.1 = (bf16[4,96,1024]{2,1,0:T(8,128)(2,1)}, bf16[4,96,1024]{2,1,0:T(8,128)(2,1)}) custom-call(s32[1]{0:T(128)} %bitcast.20.place_ref, bf16[2,4,48,2048]{3,2,1,0:T(8,128)(2,1)} %bitcast.51, bf16[16,128]{1,0:T(8,128)(2,1)} %slice_bitcast_fusion._), custom_call_target="tpu_custom_call" | custom-call | tf_op jit(solution)/shard_map/halves/pallas_call | solution.py:98
  38.6 0.6 collective-permute-start.15
  39.1 4.1 %collective-permute-start.2 = (bf16[144,1536]{1,0:T(8,128)(2,1)S(1)}, bf16[144,1536]{1,0:T(8,128)(2,1)S(1)}, u32[]{:S(2)}, u32[]{:S(2)}) collective-permute-start(bf16[144,1536]{1,0:T(8,128)(2,1)S(1)} %get-tuple-element.22), channel_id=1, source_target_pairs={{0,128},{128,0},{1,129},{129,1},{2,130},{130,2},{3,131},{131,3},{4... | collective-permute-start | bytes 1327112 | tf_op jit(solution)/shard_map/ppermute | solution.py:426
  43.3 25.4 %all-gather.5.cloned.1.call-done = bf16[16,128,256]{2,1,0:T(8,128)(2,1)} async-done(((bf16[2,128,256]{2,1,0:T(8,128)(2,1)}), bf16[16,128,256]{2,1,0:T(8,128)(2,1)}) %all-gather.5.cloned.1.call-update) | async-done | bytes 1048592 | tf_op jit(solution)/shard_map/all_gather | solution.py:418
  68.7 0.6 mark.1
  69.3 7.7 %collective-permute-done.2.p10 = bf16[144,1536]{1,0:T(8,128)(2,1)S(1)} collective-permute-done((bf16[144,1536]{1,0:T(8,128)(2,1)S(1)}, bf16[144,1536]{1,0:T(8,128)(2,1)S(1)}, u32[]{:S(2)}, u32[]{:S(2)}) %collective-permute-start.2) | collective-permute-done | bytes 442400 | tf_op jit(solution)/shard_map/ppermute | solution.py:426
  77.0 1.3 fusion.refs_0_._
  78.3 0.0 collective-permute-done.15.other_ref
  78.3 0.9 copy-done.15
  79.2 3.6 %beside.1 = bf16[2,4,96,1024]{3,2,1,0:T(8,128)(2,1)} custom-call(bf16[4,96,1024]{2,1,0:T(8,128)(2,1)} %get-tuple-element.29.keep_ref, bf16[4,96,1024]{2,1,0:T(8,128)(2,1)} %copy-done.15, bf16[16,128]{1,0:T(8,128)(2,1)} %fusion.refs_0_._), custom_call_target="tpu_custom_call" | custom-call | tf_op jit(solution)/shard_map/beside/pallas_call | solution.py:119
  82.9 0.0 all-gather.7.cloned.1.call-update
  82.9 0.1 collective-permute-start.1
  83.0 0.5 collective-permute-start.3
  83.5 0.1 pad_add_fusion.place_ref
  83.6 0.1 collective-permute-start.10
  83.7 2.0 %collective-permute-start.7 = (bf16[4,96,1536]{2,1,0:T(8,128)(2,1)}, bf16[4,96,1536]{2,1,0:T(8,128)(2,1)}, u32[]{:S(2)}, u32[]{:S(2)}) collective-permute-start(bf16[4,96,1536]{2,1,0:T(8,128)(2,1)} %bitcast.54), channel_id=1, source_target_pairs={{0,16},{16,0},{1,17},{17,1},{2,18},{18,2},{3,19},{19,3},{4,20},{20... | collective-permute-start | bytes 3538952 | tf_op jit(solution)/shard_map/ppermute | solution.py:432
  85.7 0.2 collective-permute-start.6
  85.9 0.1 collective-permute-done.3.p11
  86.0 0.8 copy-done.10
  86.8 1.0 copy-done.11
  87.8 12.6 %attention.1 = (bf16[8,2,128,256]{3,2,1,0:T(8,128)(2,1)}, f32[2,128,768]{2,1,0:T(8,128)S(1)}, bf16[2,128,768]{2,1,0:T(8,128)(2,1)S(1)}) custom-call(s32[3]{0:T(128)S(1)} %pad_add_fusion.place_ref, bf16[8,2,128,256]{3,2,1,0:T(8,128)(2,1)S(1)} %bitcast.50, bf16[144,1536]{1,0:T(8,128)(2,1)S(1)} %get-tuple-element.21.p00, ...), custom_call_target="tpu_custom_call" | custom-call | flops 16000000000 | bytes 8000000 | tf_op jit(solution)/shard_map/attention/pallas_call | solution.py:238
  100.4 0.7 copy-done.12
  101.1 14.0 %all-to-all-start.1 = ((bf16[8,2,128,256]{3,2,1,0:T(8,128)(2,1)}), bf16[8,2,128,256]{3,2,1,0:T(8,128)(2,1)S(1)}, u32[]{:S(2)}, u32[]{:S(2)}) async-start(bf16[8,2,128,256]{3,2,1,0:T(8,128)(2,1)} %get-tuple-element.24), calls=%async_computation.1 | async-start | bytes 2097152 | tf_op jit(solution)/shard_map/all_to_all | solution.py:451
  115.1 0.0 collective-permute-done.7.rows_ref.refs_2_
  115.2 2.1 %part.2 = bf16[2,96,1536]{2,1,0:T(8,128)(2,1)} custom-call(bf16[4,96,1536]{2,1,0:T(8,128)(2,1)} %collective-permute-done.7.rows_ref.refs_2_), custom_call_target="tpu_custom_call" | custom-call | flops 6000000000 | bytes 2000000 | tf_op jit(solution)/shard_map/part/pallas_call | solution.py:309
  117.3 0.6 collective-permute-start.8
  117.9 2.2 %part.3 = bf16[2,96,1536]{2,1,0:T(8,128)(2,1)} custom-call(bf16[4,96,1536]{2,1,0:T(8,128)(2,1)} %collective-permute-done.6.rows_ref.refs_1_), custom_call_target="tpu_custom_call" | custom-call | flops 6000000000 | bytes 2000000 | tf_op jit(solution)/shard_map/part/pallas_call | solution.py:309
  120.0 0.1 collective-permute-start.9
  120.2 0.1 collective-permute-start.12
  120.2 0.4 collective-permute-start.11
  120.7 12.6 %collective-permute-done.8.refs_3_ = bf16[2,96,1536]{2,1,0:T(8,128)(2,1)S(1)} collective-permute-done((bf16[2,96,1536]{2,1,0:T(8,128)(2,1)}, bf16[2,96,1536]{2,1,0:T(8,128)(2,1)S(1)}, u32[]{:S(2)}, u32[]{:S(2)}) %collective-permute-start.8) | collective-permute-done | bytes 589856 | tf_op jit(solution)/shard_map/ppermute | solution.py:434
  133.2 0.0 collective-permute-start.13
  133.2 18.1 %collective-permute-done.9.refs_4_ = bf16[2,96,1536]{2,1,0:T(8,128)(2,1)} collective-permute-done((bf16[2,96,1536]{2,1,0:T(8,128)(2,1)}, bf16[2,96,1536]{2,1,0:T(8,128)(2,1)}, u32[]{:S(2)}, u32[]{:S(2)}) %collective-permute-start.9) | collective-permute-done | bytes 589856 | tf_op jit(solution)/shard_map/ppermute | solution.py:435
  151.4 0.0 collective-permute-start.14
  151.4 0.6 pad_add_fusion.1.place_ref
  151.9 0.0 all-to-all-done.1.parts_ref
  151.9 0.2 finish.1
  152.2 0.7 copy-done.5
  152.9 0.0 collective-permute-done.10.refs_5_
  152.9 0.5 collective-permute-start.5
  153.4 0.3 collective-permute-done.14.refs_9_
  153.7 0.0 collective-permute-done.12.refs_7_
  153.7 0.0 collective-permute-done.11.refs_6_
  153.7 0.0 all-gather.7.cloned.1.call-done
  153.7 16.8 %down.1._ = bf16[1024,1536]{1,0:T(8,128)(2,1)} custom-call(s32[2]{0:T(128)} %pad_add_fusion.1.place_ref, bf16[4,96,1536]{2,1,0:T(8,128)(2,1)} %bitcast.56, bf16[4,96,1536]{2,1,0:T(8,128)(2,1)} %collective-permute-done.6.rows_ref.refs_1_, bf16[4,96,1536]{2,1,0:T(8,128)(2,1)} %collective-permute-done.7.rows_ref.refs_2_, bf16[2,96,1536]{2,1,0:T(8,128)(2,1)} %copy-done.18, ...), custom_call_target="tpu_custom_call" | custom-call | flops 16000000000 | bytes 20000000 | tf_op jit(solution)/shard_map/down/pallas_call | solution.py:340
  170.5 0.7 copy-done.16
  171.2 1.8 %spread.1 = (bf16[128,1536]{1,0:T(8,128)(2,1)}, bf16[128,256]{1,0:T(8,128)(2,1)}, bf16[128,256]{1,0:T(8,128)(2,1)}) custom-call(s32[1]{0:T(128)} %bitcast.place_ref, bf16[128,1024]{1,0:T(8,128)(2,1)} %copy-done.5, bf16[128,1024]{1,0:T(8,128)(2,1)} %copy-done.16, bf16[1024,1536]{1,0:T(8,128)(2,1)} %down.1._), custom_call_target="tpu_custom_call" | custom-call | tf_op jit(solution)/shard_map/spread/pallas_call | solution.py:392
  (36 shorter events, 0.1 us)
Async XLA Ops:
  7.2 14.7 %copy-start.8 = (s32[1,128,2]{1,2,0:T(2,128)S(1)}, s32[1,128,2]{1,2,0:T(2,128)}, u32[]{:S(2)}) copy-start(s32[1,128,2]{1,2,0:T(2,128)} %param.18) | copy-start | bytes 3076
  7.2 14.7 %copy-start.7 = (s32[1,128,2]{1,2,0:T(2,128)S(1)}, s32[1,128,2]{1,2,0:T(2,128)}, u32[]{:S(2)}) copy-start(s32[1,128,2]{1,2,0:T(2,128)} %param.17) | copy-start | bytes 3076
  7.2 14.7 %copy-start.3 = (bf16[1,128,1536]{2,1,0:T(8,128)(2,1)S(1)}, bf16[1,128,1536]{2,1,0:T(8,128)(2,1)}, u32[]{:S(2)}) copy-start(bf16[1,128,1536]{2,1,0:T(8,128)(2,1)} %param.16) | copy-start | bytes 1179652
  7.2 61.5 %all-gather.5.cloned.1.call-start = ((), (), s32[]{:S(2)}) async-start(), calls=%async_computation.2 | async-start | bytes 1179648 | tf_op jit(solution)/shard_map/all_gather | solution.py:418
  8.8 6.0 %collective-permute-start = (bf16[128,256]{1,0:T(8,128)(2,1)}, bf16[128,256]{1,0:T(8,128)(2,1)S(1)}, u32[]{:S(2)}, u32[]{:S(2)}) collective-permute-start(bf16[128,256]{1,0:T(8,128)(2,1)} %get-tuple-element.20), channel_id=1, source_target_pairs={{0,128},{128,0},{1,129},{129,1},{2,130},{130,2},{3,131},{131,3},{4... | collective-permute-start | bytes 196616 | tf_op jit(solution)/shard_map/ppermute | solution.py:417
  14.8 0.6 copy-start.17
  17.7 1.0 copy-start
  18.7 1.0 copy-start.1
  19.7 1.0 copy-start.2
  20.7 0.8 copy-start.4
  23.6 53.4 %all-to-all-start = ((bf16[8,48,1536]{2,1,0:T(8,128)(2,1)}), bf16[8,48,1536]{2,1,0:T(8,128)(2,1)S(1)}, u32[]{:S(2)}, u32[]{:S(2)}) async-start(bf16[8,48,1536]{2,1,0:T(8,128)(2,1)} %route.1), calls=%async_computation | async-start | bytes 2359296 | tf_op jit(solution)/shard_map/all_to_all | solution.py:429
  33.6 120.1 %all-gather.7.cloned.1.call-start = ((), (), s32[]{:S(2)}) async-start(), calls=%async_computation.3 | async-start | bytes 7864320 | tf_op jit(solution)/shard_map/all_gather | solution.py:444
  38.6 39.7 %collective-permute-start.15 = (bf16[4,96,1024]{2,1,0:T(8,128)(2,1)}, bf16[4,96,1024]{2,1,0:T(8,128)(2,1)S(1)}, u32[]{:S(2)}, u32[]{:S(2)}) collective-permute-start(bf16[4,96,1024]{2,1,0:T(8,128)(2,1)} %get-tuple-element.30), channel_id=1, source_target_pairs={{0,1},{1,0},{2,3},{3,2},{4,5},{5,4},{6,7},{7,6},{8,9},{9,8},{10,11... | collective-permute-start | bytes 2359304 | tf_op jit(solution)/shard_map/ppermute | solution.py:443
  39.1 37.8 %collective-permute-start.2 = (bf16[144,1536]{1,0:T(8,128)(2,1)S(1)}, bf16[144,1536]{1,0:T(8,128)(2,1)S(1)}, u32[]{:S(2)}, u32[]{:S(2)}) collective-permute-start(bf16[144,1536]{1,0:T(8,128)(2,1)S(1)} %get-tuple-element.22), channel_id=1, source_target_pairs={{0,128},{128,0},{1,129},{129,1},{2,130},{130,2},{3,131},{131,3},{4... | collective-permute-start | bytes 1327112 | tf_op jit(solution)/shard_map/ppermute | solution.py:426
  77.0 1.3 copy-start.14
  78.3 0.9 copy-start.15
  82.9 4.0 %copy-start.6 = (bf16[16,128]{1,0:T(8,128)(2,1)S(1)}, bf16[16,128]{1,0:T(8,128)(2,1)}, u32[]{:S(2)}) copy-start(bf16[16,128]{1,0:T(8,128)(2,1)} %fusion.refs_0_._) | copy-start | bytes 12292
  82.9 4.0 %copy-start.9 = (bf16[16,128,256]{2,1,0:T(8,128)(2,1)S(1)}, bf16[16,128,256]{2,1,0:T(8,128)(2,1)}, u32[]{:S(2)}) copy-start(bf16[16,128,256]{2,1,0:T(8,128)(2,1)} %all-gather.5.cloned.1.call-done) | copy-start | bytes 3145732
  82.9 3.0 %collective-permute-start.1 = (bf16[144,1536]{1,0:T(8,128)(2,1)S(1)}, bf16[144,1536]{1,0:T(8,128)(2,1)S(1)}, u32[]{:S(2)}, u32[]{:S(2)}) collective-permute-start(bf16[144,1536]{1,0:T(8,128)(2,1)S(1)} %get-tuple-element.21.p00), channel_id=1, source_target_pairs={{0,8},{8,0},{1,9},{9,1},{2,10},{10,2},{3,11},{11,3},{4,12},{12,4},... | collective-permute-start | bytes 1327112 | tf_op jit(solution)/shard_map/ppermute | solution.py:446
  83.0 3.0 %collective-permute-start.3 = (bf16[144,1536]{1,0:T(8,128)(2,1)S(1)}, bf16[144,1536]{1,0:T(8,128)(2,1)S(1)}, u32[]{:S(2)}, u32[]{:S(2)}) collective-permute-start(bf16[144,1536]{1,0:T(8,128)(2,1)S(1)} %collective-permute-done.2.p10), channel_id=1, source_target_pairs={{0,8},{8,0},{1,9},{9,1},{2,10},{10,2},{3,11},{11,3},{4,12},{12,4},... | collective-permute-start | bytes 1327112 | tf_op jit(solution)/shard_map/ppermute | solution.py:446
  83.6 69.3 %collective-permute-start.10 = (bf16[4,96,1536]{2,1,0:T(8,128)(2,1)}, bf16[4,96,1536]{2,1,0:T(8,128)(2,1)}, u32[]{:S(2)}, u32[]{:S(2)}) collective-permute-start(bf16[4,96,1536]{2,1,0:T(8,128)(2,1)} %bitcast.53), channel_id=1, source_target_pairs={{0,8},{8,0},{1,9},{9,1},{2,10},{10,2},{3,11},{11,3},{4,12},{12,4},... | collective-permute-start | bytes 3538952 | tf_op jit(solution)/shard_map/ppermute | solution.py:438
  83.7 31.5 %collective-permute-start.7 = (bf16[4,96,1536]{2,1,0:T(8,128)(2,1)}, bf16[4,96,1536]{2,1,0:T(8,128)(2,1)}, u32[]{:S(2)}, u32[]{:S(2)}) collective-permute-start(bf16[4,96,1536]{2,1,0:T(8,128)(2,1)} %bitcast.54), channel_id=1, source_target_pairs={{0,16},{16,0},{1,17},{17,1},{2,18},{18,2},{3,19},{19,3},{4,20},{20... | collective-permute-start | bytes 3538952 | tf_op jit(solution)/shard_map/ppermute | solution.py:432
  85.7 32.2 %collective-permute-start.6 = (bf16[4,96,1536]{2,1,0:T(8,128)(2,1)}, bf16[4,96,1536]{2,1,0:T(8,128)(2,1)}, u32[]{:S(2)}, u32[]{:S(2)}) collective-permute-start(bf16[4,96,1536]{2,1,0:T(8,128)(2,1)} %bitcast.55), channel_id=1, source_target_pairs={{0,1},{1,0},{2,3},{3,2},{4,5},{5,4},{6,7},{7,6},{8,9},{9,8},{10,11... | collective-permute-start | bytes 3538952 | tf_op jit(solution)/shard_map/ppermute | solution.py:431
  86.0 0.8 copy-start.10
  86.8 1.0 copy-start.11
  100.4 0.7 copy-start.12
  101.1 14.0 %copy-start.13 = (bf16[2,128,768]{2,1,0:T(8,128)(2,1)S(1)}, bf16[2,128,768]{2,1,0:T(8,128)(2,1)}, u32[]{:S(2)}) copy-start(bf16[2,128,768]{2,1,0:T(8,128)(2,1)} %copy-done.12) | copy-start | bytes 1179652
  101.1 50.8 %all-to-all-start.1 = ((bf16[8,2,128,256]{3,2,1,0:T(8,128)(2,1)}), bf16[8,2,128,256]{3,2,1,0:T(8,128)(2,1)S(1)}, u32[]{:S(2)}, u32[]{:S(2)}) async-start(bf16[8,2,128,256]{3,2,1,0:T(8,128)(2,1)} %get-tuple-element.24), calls=%async_computation.1 | async-start | bytes 2097152 | tf_op jit(solution)/shard_map/all_to_all | solution.py:451
  115.1 5.1 %collective-permute-start.4 = (bf16[2,128,768]{2,1,0:T(8,128)(2,1)S(1)}, bf16[2,128,768]{2,1,0:T(8,128)(2,1)S(1)}, u32[]{:S(2)}, u32[]{:S(2)}) collective-permute-start(bf16[2,128,768]{2,1,0:T(8,128)(2,1)S(1)} %copy-done.13), channel_id=1, source_target_pairs={{0,8},{8,0},{1,9},{9,1},{2,10},{10,2},{3,11},{11,3},{4,12},{12,4},... | collective-permute-start | bytes 1179656 | tf_op jit(solution)/shard_map/ppermute | solution.py:450
  117.3 15.9 %collective-permute-start.8 = (bf16[2,96,1536]{2,1,0:T(8,128)(2,1)}, bf16[2,96,1536]{2,1,0:T(8,128)(2,1)S(1)}, u32[]{:S(2)}, u32[]{:S(2)}) collective-permute-start(bf16[2,96,1536]{2,1,0:T(8,128)(2,1)} %part.2), channel_id=1, source_target_pairs={{0,1},{1,0},{2,3},{3,2},{4,5},{5,4},{6,7},{7,6},{8,9},{9,8},{10,11... | collective-permute-start | bytes 1769480 | tf_op jit(solution)/shard_map/ppermute | solution.py:434
  120.0 31.3 %collective-permute-start.9 = (bf16[2,96,1536]{2,1,0:T(8,128)(2,1)}, bf16[2,96,1536]{2,1,0:T(8,128)(2,1)}, u32[]{:S(2)}, u32[]{:S(2)}) collective-permute-start(bf16[2,96,1536]{2,1,0:T(8,128)(2,1)} %part.3), channel_id=1, source_target_pairs={{0,16},{16,0},{1,17},{17,1},{2,18},{18,2},{3,19},{19,3},{4,20},{20... | collective-permute-start | bytes 1769480 | tf_op jit(solution)/shard_map/ppermute | solution.py:435
  120.2 33.5 %collective-permute-start.12 = (bf16[4,96,1536]{2,1,0:T(8,128)(2,1)}, bf16[4,96,1536]{2,1,0:T(8,128)(2,1)}, u32[]{:S(2)}, u32[]{:S(2)}) collective-permute-start(bf16[4,96,1536]{2,1,0:T(8,128)(2,1)} %collective-permute-done.7.rows_ref.refs_2_), channel_id=1, source_target_pairs={{0,8},{8,0},{1,9},{9,1},{2,10},{10,2},{3,11},{11,3},{4,12},{12,4},... | collective-permute-start | bytes 3538952 | tf_op jit(solution)/shard_map/ppermute | solution.py:438
  120.2 33.5 %collective-permute-start.11 = (bf16[4,96,1536]{2,1,0:T(8,128)(2,1)}, bf16[4,96,1536]{2,1,0:T(8,128)(2,1)}, u32[]{:S(2)}, u32[]{:S(2)}) collective-permute-start(bf16[4,96,1536]{2,1,0:T(8,128)(2,1)} %collective-permute-done.6.rows_ref.refs_1_), channel_id=1, source_target_pairs={{0,8},{8,0},{1,9},{9,1},{2,10},{10,2},{3,11},{11,3},{4,12},{12,4},... | collective-permute-start | bytes 3538952 | tf_op jit(solution)/shard_map/ppermute | solution.py:438
  133.2 20.5 %copy-start.18 = (bf16[2,96,1536]{2,1,0:T(8,128)(2,1)}, bf16[2,96,1536]{2,1,0:T(8,128)(2,1)S(1)}, u32[]{:S(2)}) copy-start(bf16[2,96,1536]{2,1,0:T(8,128)(2,1)S(1)} %collective-permute-done.8.refs_3_) | copy-start | bytes 1769476
  133.2 20.1 %collective-permute-start.13 = (bf16[2,96,1536]{2,1,0:T(8,128)(2,1)S(1)}, bf16[2,96,1536]{2,1,0:T(8,128)(2,1)}, u32[]{:S(2)}, u32[]{:S(2)}) collective-permute-start(bf16[2,96,1536]{2,1,0:T(8,128)(2,1)S(1)} %collective-permute-done.8.refs_3_), channel_id=1, source_target_pairs={{0,8},{8,0},{1,9},{9,1},{2,10},{10,2},{3,11},{11,3},{4,12},{12,4},... | collective-permute-start | bytes 1769480 | tf_op jit(solution)/shard_map/ppermute | solution.py:438
  151.4 2.3 %collective-permute-start.14 = (bf16[2,96,1536]{2,1,0:T(8,128)(2,1)}, bf16[2,96,1536]{2,1,0:T(8,128)(2,1)}, u32[]{:S(2)}, u32[]{:S(2)}) collective-permute-start(bf16[2,96,1536]{2,1,0:T(8,128)(2,1)} %collective-permute-done.9.refs_4_), channel_id=1, source_target_pairs={{0,8},{8,0},{1,9},{9,1},{2,10},{10,2},{3,11},{11,3},{4,12},{12,4},... | collective-permute-start | bytes 1769480 | tf_op jit(solution)/shard_map/ppermute | solution.py:438
  152.2 0.7 copy-start.5
  152.9 17.6 %collective-permute-start.5 = (bf16[128,1024]{1,0:T(8,128)(2,1)S(1)}, bf16[128,1024]{1,0:T(8,128)(2,1)S(1)}, u32[]{:S(2)}, u32[]{:S(2)}) collective-permute-start(bf16[128,1024]{1,0:T(8,128)(2,1)S(1)} %get-tuple-element.28), channel_id=1, source_target_pairs={{0,128},{128,0},{1,129},{129,1},{2,130},{130,2},{3,131},{131,3},{4... | collective-permute-start | bytes 786440 | tf_op jit(solution)/shard_map/ppermute | solution.py:456
  170.5 0.7 copy-start.16
Sparse Core Ops, SparseCore 0:
  17.1 51.4 all-gather.4
  83.0 67.0 all-gather.6
